TPU v7x, 512 devices: a whole 4x4x16 slice. The times are simulated.
512 devices in a mesh: cells: 128 (over x, z, core), comp: 4 (over y).
Axes of the slice: x: 4, y: 4, z: 16, core: 2. Of those that a mesh axis runs over, the one named last changes fastest.
Arguments:
- fine_moments: bfloat16 [288, 65536], P(None, 'cells'), may hold values from -6 to 6
- translations: bfloat16 [16, 288, 288], P('comp'), may hold values from -0.09375 to 0.09375
- shifts_up: bfloat16 [8, 288, 288], replicated, may hold values from -0.375 to 0.375
- fine_pairs: int32 [3, 16, 98304], P(None, 'comp', 'cells'), may hold values from 0 to 511, as said below
- coarse_pairs: int32 [3, 16, 98304], P(None, 'comp', 'cells'), may hold values from 0 to 127, as said below
- child_links: int32 [2, 65536], P(None, 'cells'), may hold values from 0 to 16383, as said below
Outputs:
- fine_locals: float32 [288, 65536], P('comp', 'cells')
- coarse_moments: bfloat16 [288, 16384], P(None, 'cells')
- coarse_locals: float32 [288, 16384], P('comp', 'cells')
Inputs may be any that keep to these rules, and one draw needn't show every extreme that they name: `fine_pairs`: For every pair of owners and every class at most 6 slots are live; some such block is full in every draw. `coarse_pairs`: as for fine_pairs, with coarse cells. `child_links`: row 0 is the parent coarse cell of each fine cell, never falling along the fine cells; every coarse cell has 1 to 8 children; the parents of one device's fine cells are that device's coarse cells, except that at most its last 4 fine cells may belong to the first coarse cell of the next device. Row 1 is the child's octant, 0 to 7, distinct among the children of one parent.
All inputs are finite; a program needn't handle non-finite values.
Results may differ from a plain program's by a relative error of at most 0.005.
Values may be sent and summed in bfloat16 or wider, within the bound.
No kernel may reach another device: no remote copies, remote signals or barrier semaphores. Data moves between devices by JAX's collectives and lax.ppermute only.
A program may use at most 128 MiB of HBM per device.

v0:
```python
import jax
import jax.numpy as jnp
from jax import lax
from jax.sharding import PartitionSpec as P


def passed_along(block, axis, distance):
    devices = range(lax.axis_size(axis))
    route = [(i - distance, i) for i in devices if i - distance in devices]
    return lax.ppermute(block, axis, route)


def level_pass(moments, translations, pair_list, level_scale):
    width, cells = moments.shape
    classes = pair_list.shape[1]
    slots = pair_list.shape[2]
    first_cells = pair_list[0]
    second_cells = pair_list[1]
    live_flags = pair_list[2]
    live_factor = live_flags.astype(jnp.float32)[None, :, :] * level_scale
    near_rows = jnp.take(moments, first_cells.reshape(-1), axis=1).reshape(width, classes, slots)
    near_rows = near_rows * live_flags.astype(jnp.bfloat16)[None, :, :]
    asked_cells = lax.all_to_all(second_cells, "cells", split_axis=1, concat_axis=1, tiled=True)
    answer = jnp.take(moments, asked_cells.reshape(-1), axis=1).reshape(width, classes, slots)
    far_rows = lax.all_to_all(answer, "cells", split_axis=2, concat_axis=2, tiled=True)
    to_second = (
        jnp.einsum("oij,jos->ios", translations, near_rows, preferred_element_type=jnp.float32)
        * level_scale
    )
    arrived = lax.all_to_all(
        to_second.astype(jnp.bfloat16), "cells", split_axis=2, concat_axis=2, tiled=True
    ).astype(to_second.dtype)
    to_first = (
        jnp.einsum("oji,jos->ios", translations, far_rows, preferred_element_type=jnp.float32)
        * live_factor
    )
    gathered = jnp.zeros((width, cells), jnp.float32)
    gathered = gathered.at[:, first_cells.reshape(-1)].add(to_first.reshape(width, classes * slots))
    gathered = gathered.at[:, asked_cells.reshape(-1)].add(arrived.reshape(width, classes * slots))
    return lax.psum_scatter(gathered, "comp", scatter_dimension=0, tiled=True)


def per_device(fine_moments, translations, shifts_up, fine_pairs, coarse_pairs, child_links):
    fine_locals = level_pass(fine_moments, translations, fine_pairs, 1.0)
    width, fine_cells = fine_moments.shape
    coarse_dev = fine_cells // 4
    group = lax.axis_index("cells")
    parent_local = child_links[0] - group * coarse_dev
    octant = child_links[1]
    inside = parent_local < coarse_dev
    slot_index = jnp.where(inside, octant * coarse_dev + parent_local, 8 * coarse_dev)
    placed = (
        jnp.zeros((width, 8 * coarse_dev), jnp.bfloat16)
        .at[:, slot_index]
        .set(fine_moments, mode="drop")
    )
    edge_index = jnp.where(inside, 8, octant)
    edge_part = jnp.zeros((width, 8), jnp.bfloat16).at[:, edge_index].set(fine_moments, mode="drop")
    summed = jnp.einsum(
        "ofi,ioc->fc",
        shifts_up,
        placed.reshape(width, 8, coarse_dev),
        preferred_element_type=jnp.float32,
    )
    edge_sum = jnp.einsum("ofi,io->f", shifts_up, edge_part, preferred_element_type=jnp.float32)
    incoming = passed_along(edge_sum, "cells", 1)
    summed = summed.at[:, 0].add(incoming)
    coarse_moments = summed.astype(jnp.bfloat16)
    coarse_locals = level_pass(coarse_moments, translations, coarse_pairs, 0.5)
    return (fine_locals, coarse_moments, coarse_locals)


def solution(mesh):
    return jax.shard_map(
        per_device,
        mesh=mesh,
        in_specs=(
            P(None, "cells"),
            P("comp", None, None),
            P(),
            P(None, "comp", "cells"),
            P(None, "comp", "cells"),
            P(None, "cells"),
        ),
        out_specs=(P("comp", "cells"), P(None, "cells"), P("comp", "cells")),
        check_vma=False,
    )
```

profile of v0, /device:TPU:6, one launch (start us, length us, event | category | flops | bytes accessed | tf_op | source)
XLA Modules:
  0.0 680.2 jit_solution(9049176294268324721)
XLA Ops:
  9.1 19.9 %all-to-all-start = ((s32[4,128,6]{2,0,1:T(4,128)}), s32[4,128,6]{2,0,1:T(4,128)S(1)}, u32[]{:S(2)}, u32[]{:S(2)}) async-start(s32[4,128,6]{2,0,1:T(4,128)} %copy.84), calls=%async_computation | async-start | bytes 524288 | tf_op jit(solution)/shard_map/all_to_all | solution.py:23
  30.3 13.0 %gather_fusion.1 = bf16[3072,288]{1,0:T(8,128)(2,1)} fusion(bf16[288,512]{0,1:T(8,128)(2,1)S(1)} %copy.86, s32[3072]{0:T(1024)S(1)} %fusion.26), kind=kCustom, calls=%fused_computation.2.clone | custom fusion | bytes 3551232 | tf_op jit(solution)/shard_map/jit(_take)/gather | solution.py:21
  54.2 16.6 %all-to-all-start.3 = ((s32[4,128,6]{2,0,1:T(4,128)}), s32[4,128,6]{2,0,1:T(4,128)}, u32[]{:S(2)}, u32[]{:S(2)}) async-start(s32[4,128,6]{2,0,1:T(4,128)} %copy.104), calls=%async_computation.3 | async-start | bytes 524288 | tf_op jit(solution)/shard_map/all_to_all | solution.py:23
  79.9 12.1 %all-to-all-done.3 = s32[4,128,6]{2,0,1:T(4,128)} async-done(((s32[4,128,6]{2,0,1:T(4,128)}), s32[4,128,6]{2,0,1:T(4,128)}, u32[]{:S(2)}, u32[]{:S(2)}) %all-to-all-start.3) | async-done | bytes 12320 | tf_op jit(solution)/shard_map/all_to_all | solution.py:23
  92.0 9.3 %all-to-all-start.2 = ((bf16[288,4,768]{0,1,2:T(4,128)(2,1)}), bf16[288,4,768]{0,1,2:T(4,128)(2,1)}, u32[]{:S(2)}, u32[]{:S(2)}) async-start(bf16[288,4,768]{0,1,2:T(4,128)(2,1)} %copy.96), calls=%async_computation.2 | async-start | bytes 4718592 | tf_op jit(solution)/shard_map/all_to_all | solution.py:30
  114.2 86.9 %collective-permute-done = f32[288]{0:T(512)S(1)} collective-permute-done((f32[288]{0:T(512)S(1)}, f32[288]{0:T(512)S(1)}, u32[]{:S(2)}, u32[]{:S(2)}) %collective-permute-start) | collective-permute-done | bytes 1184 | tf_op jit(solution)/shard_map/ppermute | solution.py:10
  202.6 13.1 %gather_fusion.3 = bf16[3072,288]{1,0:T(8,128)(2,1)} fusion(bf16[288,128]{0,1:T(8,128)(2,1)S(1)} %copy.106, s32[3072]{0:T(1024)S(1)} %fusion.28), kind=kCustom, calls=%fused_computation.3.clone | custom fusion | bytes 3551232 | tf_op jit(solution)/shard_map/jit(_take)/gather | solution.py:21
  232.7 18.4 %all-to-all-start.5 = ((bf16[288,4,768]{0,1,2:T(4,128)(2,1)}), bf16[288,4,768]{0,1,2:T(4,128)(2,1)}, u32[]{:S(2)}, u32[]{:S(2)}) async-start(bf16[288,4,768]{0,1,2:T(4,128)(2,1)} %copy.116), calls=%async_computation.5 | async-start | bytes 4718592 | tf_op jit(solution)/shard_map/all_to_all | solution.py:30
  252.2 13.0 %gather_fusion.2 = bf16[3072,288]{1,0:T(8,128)(2,1)} fusion(bf16[288,128]{0,1:T(8,128)(2,1)S(1)} %copy.106, s32[3072]{0:T(1024)S(1)} %fusion.27), kind=kCustom, calls=%fused_computation.1.clone | custom fusion | bytes 3551232 | tf_op jit(solution)/shard_map/jit(_take)/gather | solution.py:24
  271.4 87.8 %all-to-all-done.5 = bf16[288,4,768]{0,1,2:T(4,128)(2,1)} async-done(((bf16[288,4,768]{0,1,2:T(4,128)(2,1)}), bf16[288,4,768]{0,1,2:T(4,128)(2,1)}, u32[]{:S(2)}, u32[]{:S(2)}) %all-to-all-start.5) | async-done | bytes 1769504 | tf_op jit(solution)/shard_map/all_to_all | solution.py:30
  359.2 11.1 %all-to-all-start.4 = ((bf16[288,4,768]{0,1,2:T(4,128)(2,1)}), bf16[288,4,768]{0,1,2:T(4,128)(2,1)}, u32[]{:S(2)}, u32[]{:S(2)}) async-start(bf16[288,4,768]{0,1,2:T(4,128)(2,1)} %copy.108), calls=%async_computation.4 | async-start | bytes 4718592 | tf_op jit(solution)/shard_map/all_to_all | solution.py:25
  370.5 13.0 %gather_fusion = bf16[3072,288]{1,0:T(8,128)(2,1)} fusion(bf16[288,512]{0,1:T(8,128)(2,1)S(1)} %copy.86, s32[3072]{0:T(1024)S(1)} %fusion.25), kind=kCustom, calls=%fused_computation.clone | custom fusion | bytes 3551232 | tf_op jit(solution)/shard_map/jit(_take)/gather | solution.py:24
  389.7 88.7 %all-to-all-done.4 = bf16[288,4,768]{0,1,2:T(4,128)(2,1)} async-done(((bf16[288,4,768]{0,1,2:T(4,128)(2,1)}), bf16[288,4,768]{0,1,2:T(4,128)(2,1)}, u32[]{:S(2)}, u32[]{:S(2)}) %all-to-all-start.4) | async-done | bytes 1769504 | tf_op jit(solution)/shard_map/all_to_all | solution.py:25
  478.4 11.1 %all-to-all-start.1 = ((bf16[288,4,768]{0,1,2:T(4,128)(2,1)}), bf16[288,4,768]{0,1,2:T(4,128)(2,1)}, u32[]{:S(2)}, u32[]{:S(2)}) async-start(bf16[288,4,768]{0,1,2:T(4,128)(2,1)} %copy.88), calls=%async_computation.1 | async-start | bytes 4718592 | tf_op jit(solution)/shard_map/all_to_all | solution.py:25
  496.9 5.5 copy.99
  508.9 5.6 copy.119
  519.4 5.5 copy.112
  524.9 19.2 %scatter_custom_fusion.4 = f32[288,128]{0,1:T(8,128)S(1)} fusion(s32[3072]{0:T(1024)S(1)} %bitcast.105, f32[3072,288]{1,0:T(8,128)} %copy.112, f32[]{:T(128)} %constant.67.clone.1), kind=kCustom, calls=%fused_computation.36 | custom fusion | flops 884736 | bytes 147968 | tf_op jit(solution)/shard_map/scatter-add | solution.py:38
  544.1 19.2 %scatter_fusion.1 = f32[288,128]{0,1:T(8,128)S(1)} fusion(f32[288,128]{0,1:T(8,128)S(1)} %scatter_custom_fusion.4, s32[3072]{0:T(1024)S(1)} %bitcast.103, f32[3072,288]{1,0:T(8,128)} %copy.119), kind=kCustom, calls=%fused_computation.9 | custom fusion | flops 884736 | bytes 10629120 | tf_op jit(solution)/shard_map/scatter-add | solution.py:39
  564.4 33.2 %all-to-all-done.1 = bf16[288,4,768]{0,1,2:T(4,128)(2,1)} async-done(((bf16[288,4,768]{0,1,2:T(4,128)(2,1)}), bf16[288,4,768]{0,1,2:T(4,128)(2,1)}, u32[]{:S(2)}, u32[]{:S(2)}) %all-to-all-start.1) | async-done | bytes 1769504 | tf_op jit(solution)/shard_map/all_to_all | solution.py:25
  602.6 5.6 copy.92
  608.1 19.3 %scatter_custom_fusion = f32[288,512]{0,1:T(8,128)S(1)} fusion(s32[3072]{0:T(1024)S(1)} %bitcast.104, f32[3072,288]{1,0:T(8,128)} %copy.92, f32[]{:T(128)} %constant.67.clone.1), kind=kCustom, calls=%fused_computation.33 | custom fusion | flops 884736 | bytes 590336 | tf_op jit(solution)/shard_map/scatter-add | solution.py:38
  627.5 19.5 %scatter_fusion = f32[288,512]{0,1:T(8,128)S(1)} fusion(f32[288,512]{0,1:T(8,128)S(1)} %scatter_custom_fusion, s32[3072]{0:T(1024)S(1)} %bitcast.102, f32[3072,288]{1,0:T(8,128)} %copy.99), kind=kCustom, calls=%fused_computation.5 | custom fusion | flops 884736 | bytes 10629120 | tf_op jit(solution)/shard_map/scatter-add | solution.py:39
  651.7 21.1 %reduce-scatter.5.cloned.1.call-done = f32[72,512]{1,0:T(8,128)} async-done(((f32[288,512]{1,0:T(8,128)}), f32[72,512]{1,0:T(8,128)}) %reduce-scatter.5.cloned.1.call-update) | async-done | bytes 147472
  (97 shorter events, 96.7 us)
Async XLA Ops:
  7.2 97.9 %copy-start = (bf16[8,288,288]{2,1,0:T(8,128)(2,1)S(1)}, bf16[8,288,288]{2,1,0:T(8,128)(2,1)}, u32[]{:S(2)}) copy-start(bf16[8,288,288]{2,1,0:T(8,128)(2,1)} %param.14) | copy-start | bytes 3981316
  9.1 45.1 %all-to-all-start = ((s32[4,128,6]{2,0,1:T(4,128)}), s32[4,128,6]{2,0,1:T(4,128)S(1)}, u32[]{:S(2)}, u32[]{:S(2)}) async-start(s32[4,128,6]{2,0,1:T(4,128)} %copy.84), calls=%async_computation | async-start | bytes 524288 | tf_op jit(solution)/shard_map/all_to_all | solution.py:23
  43.3 3.9 copy-start.8
  47.3 23.6 %copy-start.3 = (bf16[4,288,288]{2,1,0:T(8,128)(2,1)S(1)}, bf16[4,288,288]{2,1,0:T(8,128)(2,1)}, u32[]{:S(2)}) copy-start(bf16[4,288,288]{2,1,0:T(8,128)(2,1)} %param.13) | copy-start | bytes 1990660
  54.2 20.5 %copy-start.5 = (s32[4,128,6]{2,0,1:T(4,128)}, s32[4,128,6]{2,0,1:T(4,128)S(1)}, u32[]{:S(2)}) copy-start(s32[4,128,6]{2,0,1:T(4,128)S(1)} %all-to-all-done) | copy-start | bytes 36868
  54.2 37.8 %all-to-all-start.3 = ((s32[4,128,6]{2,0,1:T(4,128)}), s32[4,128,6]{2,0,1:T(4,128)}, u32[]{:S(2)}, u32[]{:S(2)}) async-start(s32[4,128,6]{2,0,1:T(4,128)} %copy.104), calls=%async_computation.3 | async-start | bytes 524288 | tf_op jit(solution)/shard_map/all_to_all | solution.py:23
  79.9 21.4 %copy-start.4 = (bf16[288,512]{1,0:T(8,128)(2,1)S(1)}, bf16[288,512]{1,0:T(8,128)(2,1)}, u32[]{:S(2)}) copy-start(bf16[288,512]{1,0:T(8,128)(2,1)} %param.12) | copy-start | bytes 884740
  79.9 22.4 %copy-start.9 = (s32[2,512]{1,0:T(2,128)S(1)}, s32[2,512]{1,0:T(2,128)}, u32[]{:S(2)}) copy-start(s32[2,512]{1,0:T(2,128)} %param.17) | copy-start | bytes 12292
  92.0 140.7 %all-to-all-start.2 = ((bf16[288,4,768]{0,1,2:T(4,128)(2,1)}), bf16[288,4,768]{0,1,2:T(4,128)(2,1)}, u32[]{:S(2)}, u32[]{:S(2)}) async-start(bf16[288,4,768]{0,1,2:T(4,128)(2,1)} %copy.96), calls=%async_computation.2 | async-start | bytes 4718592 | tf_op jit(solution)/shard_map/all_to_all | solution.py:30
  105.6 95.5 %collective-permute-start = (f32[288]{0:T(512)S(1)}, f32[288]{0:T(512)S(1)}, u32[]{:S(2)}, u32[]{:S(2)}) collective-permute-start(f32[288]{0:T(512)S(1)} %convolution_reduce_fusion), channel_id=1, source_target_pairs={{0,4},{4,8},{8,12},{12,16},{16,20},{20,24},{24,28},{28,32},{32,36}... | collective-permute-start | bytes 3464 | tf_op jit(solution)/shard_map/ppermute | solution.py:10
  202.4 13.2 %copy-start.7 = (bf16[288,128]{1,0:T(8,128)(2,1)}, bf16[288,128]{1,0:T(8,128)(2,1)S(1)}, u32[]{:S(2)}) copy-start(bf16[288,128]{1,0:T(8,128)(2,1)S(1)} %convert_element_type.37) | copy-start | bytes 221188
  232.7 126.5 %all-to-all-start.5 = ((bf16[288,4,768]{0,1,2:T(4,128)(2,1)}), bf16[288,4,768]{0,1,2:T(4,128)(2,1)}, u32[]{:S(2)}, u32[]{:S(2)}) async-start(bf16[288,4,768]{0,1,2:T(4,128)(2,1)} %copy.116), calls=%async_computation.5 | async-start | bytes 4718592 | tf_op jit(solution)/shard_map/all_to_all | solution.py:30
  271.4 98.9 %copy-start.6 = (s32[4,128,6]{2,0,1:T(4,128)S(1)}, s32[4,128,6]{2,0,1:T(4,128)}, u32[]{:S(2)}) copy-start(s32[4,128,6]{2,0,1:T(4,128)} %copy-done.5) | copy-start | bytes 36868
  359.2 119.2 %all-to-all-start.4 = ((bf16[288,4,768]{0,1,2:T(4,128)(2,1)}), bf16[288,4,768]{0,1,2:T(4,128)(2,1)}, u32[]{:S(2)}, u32[]{:S(2)}) async-start(bf16[288,4,768]{0,1,2:T(4,128)(2,1)} %copy.108), calls=%async_computation.4 | async-start | bytes 4718592 | tf_op jit(solution)/shard_map/all_to_all | solution.py:25
  478.4 119.2 %all-to-all-start.1 = ((bf16[288,4,768]{0,1,2:T(4,128)(2,1)}), bf16[288,4,768]{0,1,2:T(4,128)(2,1)}, u32[]{:S(2)}, u32[]{:S(2)}) async-start(bf16[288,4,768]{0,1,2:T(4,128)(2,1)} %copy.88), calls=%async_computation.1 | async-start | bytes 4718592 | tf_op jit(solution)/shard_map/all_to_all | solution.py:25
  489.5 160.5 %all-reduce.3.cloned.1.call-start = ((), (), s32[]{:S(2)}) async-start(), calls=%async_computation.8 | async-start | bytes 393216
  563.4 0.7 copy-start.2
  564.1 108.8 %reduce-scatter.5.cloned.1.call-start = ((), (), s32[]{:S(2)}) async-start(), calls=%async_computation.7 | async-start | bytes 737280
  627.5 45.4 %copy-start.1 = (bf16[8,288,288]{2,1,0:T(8,128)(2,1)S(1)}, bf16[8,288,288]{2,1,0:T(8,128)(2,1)}, u32[]{:S(2)}) copy-start(bf16[8,288,288]{2,1,0:T(8,128)(2,1)} %param.14) | copy-start | bytes 3981316
Sparse Core Ops, SparseCore 0:
  564.2 57.5 all-reduce.2
  648.2 24.5 reduce-scatter.4
where the time goes:
time: 691 us; the launch traced here: 680 us
  waiting for transfers between devices  330 us (48%)
  local copies, waits for them, and re-layouts  136 us (20%)
  other arithmetic  93.7 us (14%)
  starting transfers between devices  89.4 us (13%)
  between operations  15.7 us (2%)
  matrix products  15.6 us (2%)
    all_to_all x2, waiting for transfers between devices, level_pass(): lax.all_to_all(answer, 'cells', split_axis=2, concat_axis=2, tiled=True)  122 us
    all_to_all x2, waiting for transfers between devices, level_pass(): lax.all_to_all(to_second.astype(jnp.bfloat16), 'cells', split_axis=2, con...  87.8 us
    ppermute x1, waiting for transfers between devices, passed_along(): return lax.ppermute(block, axis, route)  86.9 us
    scatter-add x2, other arithmetic, level_pass(): gathered.at[:, asked_cells.reshape(-1)]  38.7 us
    scatter-add x2, other arithmetic, level_pass(): gathered.at[:, first_cells.reshape(-1)]  38.5 us
    all_to_all x2, starting transfers between devices, level_pass(): lax.all_to_all(second_cells, 'cells', split_axis=1, concat_axis=1, tiled=...  36.6 us
    all_to_all x2, starting transfers between devices, level_pass(): lax.all_to_all(to_second.astype(jnp.bfloat16), 'cells', split_axis=2, con...  27.7 us
    gather x2, local copies, waits for them, and re-layouts, level_pass(): jnp.take(moments, first_cells.reshape(-1), axis=1)  26.1 us
  transfers between devices with their start and end apart: 9, of which 6 were waited for; matrix products, arithmetic and copies ran while one was open for 36% of the time, Pallas kernels for 0%

commit v1 on v0

v1 whole, which is shorter than its diff:
```python
import functools

import jax
import jax.numpy as jnp
from jax import lax
from jax.experimental import pallas as pl
from jax.experimental.pallas import tpu as pltpu
from jax.sharding import Mesh
from jax.sharding import PartitionSpec as P

CAP = 6
CELLS = ("x", "zh", "zl", "core")
BF16 = jnp.bfloat16
F32 = jnp.float32


def upward_kernel(moments_ref, slot_ref, shifts_ref, out_ref):
    octants, width, _ = shifts_ref.shape
    coarse = out_ref.shape[1]
    spots = octants * coarse
    rows = lax.broadcasted_iota(jnp.int32, (spots, slot_ref.shape[1]), 0)
    hot = (rows == slot_ref[0:1, :]).astype(BF16)
    placed = lax.dot_general(
        moments_ref[...], hot, (((1,), (1,)), ((), ())), preferred_element_type=F32
    ).astype(BF16)
    total = jnp.zeros((width, coarse), F32)
    for octant in range(octants):
        part = placed[:, octant * coarse : (octant + 1) * coarse]
        total = total + jnp.dot(shifts_ref[octant], part, preferred_element_type=F32)
    out_ref[...] = total.astype(BF16)


def upward(moments, child_links, shifts_up):
    width, fine = moments.shape
    coarse = fine // 4
    group = lax.axis_index(CELLS)
    devices = lax.axis_size(CELLS)
    parent = child_links[0] - group * coarse
    octant = child_links[1]
    inside = parent < coarse
    slot = jnp.where(inside, octant * coarse + parent, -1)
    code = jnp.where(inside, -1, octant)[-4:].astype(F32)
    edge = jnp.concatenate([moments[:, -4:].T.astype(F32), code[:, None]], axis=1)
    edge = lax.ppermute(edge, CELLS, [(i, i + 1) for i in range(devices - 1)])
    edge_code = edge[:, width].astype(jnp.int32)
    edge_slot = jnp.where(edge_code >= 0, edge_code * coarse, -1)
    edge_moments = edge[:, :width].T.astype(BF16)
    pad = 124
    slots = jnp.concatenate([slot, edge_slot, jnp.full((pad,), -1, jnp.int32)])
    extended = jnp.concatenate([moments, edge_moments, jnp.zeros((width, pad), BF16)], axis=1)
    return pl.pallas_call(
        upward_kernel,
        out_shape=jax.ShapeDtypeStruct((width, coarse), BF16),
        compiler_params=pltpu.CompilerParams(vmem_limit_bytes=48 * 1024 * 1024),
        cost_estimate=pl.CostEstimate(flops=8 * 10**8, bytes_accessed=2 * 10**6, transcendentals=0),
        name="upward",
    )(extended, slots.reshape(1, -1), shifts_up)


def level_kernel(core_ref, own_ref, other_ref, src_ref, dst_ref, ops_ref, out_ref, xt_ref, s_ref, *, scale):
    step = pl.program_id(0)
    height, cells = own_ref.shape[1:]
    owners = dst_ref.shape[1]
    z = (step % 4) * 4 + step // 4
    core = core_ref[0]
    cell = lax.broadcasted_iota(jnp.int32, (cells, 128), 0)
    for block_ref, side in ((own_ref, core), (other_ref, 1 - core)):
        index = src_ref[0, side]
        hot = jnp.concatenate(
            [(cell == index[s : s + 1, :]).astype(BF16) for s in range(CAP)], axis=1
        )
        picked = jnp.dot(block_ref[0], hot, preferred_element_type=F32)
        for s in range(CAP):
            row = ((z * 2 + side) * CAP + s) * 128
            xt_ref[pl.ds(pl.multiple_of(row, 128), 128), 0:height] = picked[:, s * 128 : (s + 1) * 128].T

    @pl.when(step == pl.num_programs(0) - 1)
    def _():
        target = lax.broadcasted_iota(jnp.int32, (cells, owners), 0)

        def pair(p, carry):
            rows = dst_ref[pl.ds(pl.multiple_of(p * 8, 8), 8), :]
            for g in range(4):
                parts = []
                for j in (g, 4 + g):
                    terms = xt_ref[pl.ds(p * 8 + j, owners, stride=128), :]
                    terms = terms.T[0:height].astype(BF16)
                    hot = (target == rows[j : j + 1, :]).astype(BF16)
                    parts.append(
                        lax.dot_general(
                            terms, hot, (((1,), (1,)), ((), ())), preferred_element_type=F32
                        )
                    )
                start = pl.multiple_of(p * (2 * height), 2 * height)
                s_ref[g, pl.ds(start, 2 * height), :] = jnp.concatenate(parts, axis=0).astype(BF16)
            return carry

        lax.fori_loop(0, 16, pair, 0)
        for g in range(4):
            total = jnp.dot(ops_ref[...], s_ref[g], preferred_element_type=F32)
            out_ref[g] = (total * scale).astype(BF16)


def spread_along_z(block):
    def spread(array, axis):
        copies = jnp.broadcast_to(array[None], (4,) + array.shape)
        return lax.all_to_all(copies, axis, 0, 0, tiled=True)

    own = spread(spread(block, "zh"), "zl")
    own = own.reshape((16,) + block.shape)
    other = lax.ppermute(own, "core", [(0, 1), (1, 0)])
    return own, other


def level_partial(moments, src, dst, operators, scale):
    width, cells = moments.shape
    height = width // 4
    rows = lax.dynamic_slice_in_dim(moments, lax.axis_index("comp") * height, height, 0)
    own, other = spread_along_z(rows)
    core = lax.axis_index("core").reshape(1)
    owners = dst.shape[1]
    return pl.pallas_call(
        functools.partial(level_kernel, scale=scale),
        grid=(16,),
        in_specs=[
            pl.BlockSpec(memory_space=pltpu.SMEM),
            pl.BlockSpec((1, height, cells), lambda i: (i, 0, 0)),
            pl.BlockSpec((1, height, cells), lambda i: (i, 0, 0)),
            pl.BlockSpec((1, 2, 8, 128), lambda i: ((i % 4) * 4 + i // 4, 0, 0, 0)),
            pl.BlockSpec(dst.shape, lambda i: (0, 0)),
            pl.BlockSpec(operators.shape, lambda i: (0, 0)),
        ],
        out_specs=pl.BlockSpec((4, width, cells), lambda i: (0, 0, 0)),
        out_shape=jax.ShapeDtypeStruct((4, width, cells), BF16),
        scratch_shapes=[
            pltpu.VMEM((owners * 128, 128), F32),
            pltpu.VMEM((4, 32 * height, cells), BF16),
        ],
        compiler_params=pltpu.CompilerParams(vmem_limit_bytes=56 * 1024 * 1024),
        cost_estimate=pl.CostEstimate(flops=3 * 10**9, bytes_accessed=6 * 10**6, transcendentals=0),
        name="level",
    )(core, own, other, src, dst, operators)


def summed_over_parts(partial):
    groups, width, cells = partial.shape
    pieces = partial.reshape(groups * 4, width // 4, cells)
    pieces = lax.all_to_all(pieces, ("x", "comp"), 0, 0, tiled=True)
    return jnp.sum(pieces.astype(F32), axis=0)


def slot_lists(fine_pairs, coarse_pairs):
    both = jnp.stack([fine_pairs, coarse_pairs])
    first, second, alive = both[:, 0], both[:, 1], both[:, 2] == 1
    classes = first.shape[1]
    near = jnp.stack([jnp.where(alive, second, -1), first], axis=1)
    near = near.reshape(4 * classes, 4, 192).transpose(1, 0, 2)
    near = lax.all_to_all(near, "x", 0, 0, tiled=True)
    far = jnp.stack([jnp.where(alive, first, -1), second], axis=1)
    far = far.reshape(2, 2, classes, 4, 32, CAP).transpose(4, 0, 1, 2, 3, 5).reshape(32, 3, 128)
    far = lax.all_to_all(far, ("zh", "zl", "core"), 0, 0, tiled=True)
    gathered = lax.all_gather(
        jnp.concatenate([near.reshape(-1, 128), far.reshape(-1, 128)]), "comp"
    )
    near = gathered[:, :96].reshape(4, 4, 2, 2, classes, 192)
    far = gathered[:, 96:].reshape(4, 32, 2, 2, classes, 4, CAP)
    near_src = near[:, :, :, 0].transpose(2, 4, 0, 3, 1).reshape(2, 32, CAP, 64)
    near_dst = near[:, :, :, 1].transpose(2, 0, 3, 1, 4).reshape(2, 64, 192)
    far_src = far[:, :, :, 0].transpose(2, 1, 5, 0, 3, 4).reshape(2, 32, CAP, 64)
    far_dst = far[:, :, :, 1].transpose(2, 0, 3, 4, 1, 5).reshape(2, 64, 192)
    src = jnp.concatenate([near_src, far_src], axis=3)
    src = jnp.pad(src, ((0, 0), (0, 0), (0, 8 - CAP), (0, 0)), constant_values=-1)
    src = src.reshape(2, 16, 2, 8, 128)
    dst = jnp.concatenate([near_dst, far_dst], axis=1)
    return src, dst


def operator_columns(translations):
    width = translations.shape[1]
    height = width // 4
    every = lax.all_gather(translations, "comp", tiled=True)
    start = lax.axis_index("comp") * height
    to_first = lax.dynamic_slice_in_dim(every, start, height, 1).transpose(2, 0, 1)
    to_second = lax.dynamic_slice_in_dim(every, start, height, 2).transpose(1, 0, 2)
    return jnp.concatenate([to_first.reshape(width, -1), to_second.reshape(width, -1)], axis=1)


def per_device(fine_moments, translations, shifts_up, fine_pairs, coarse_pairs, child_links):
    src, dst = slot_lists(fine_pairs, coarse_pairs)
    operators = operator_columns(translations)
    coarse_moments = upward(fine_moments, child_links, shifts_up)
    fine_partial = level_partial(fine_moments, src[0], dst[0], operators, 1.0)
    coarse_partial = level_partial(coarse_moments, src[1], dst[1], operators, 0.5)
    return (summed_over_parts(fine_partial), coarse_moments, summed_over_parts(coarse_partial))


def solution(mesh):
    split = Mesh(mesh.devices.reshape(4, 4, 4, 2, 4), CELLS + ("comp",))
    return jax.shard_map(
        per_device,
        mesh=split,
        in_specs=(
            P(None, CELLS),
            P("comp", None, None),
            P(),
            P(None, "comp", CELLS),
            P(None, "comp", CELLS),
            P(None, CELLS),
        ),
        out_specs=(P("comp", CELLS), P(None, CELLS), P("comp", CELLS)),
        check_vma=False,
    )
```

time: 691 us -> 251 us (0.36)
  waiting for transfers between devices: 330 us -> 43.6 us
  local copies, waits for them, and re-layouts: 136 us -> 34 us
  other arithmetic: 93.7 us -> 6.37 us
  Pallas kernels: 0 us -> 59.4 us
  starting transfers between devices: 89.4 us -> 52.9 us
  blocking collectives: 0 us -> 35.9 us
  matrix products: 15.6 us -> 0 us
    all_to_all x6 -> x7, waiting for transfers between devices: 222 us -> 41.3 us  [the longest x2 15.5 us: summed_over_parts(): pieces = lax.all_to_all(pieces, ('x', 'comp'), 0, 0, tiled=True)]
    ppermute x1 -> x3, waiting for transfers between devices: 86.9 us -> 0.01 us  [the longest x2 0.01 us: spread_along_z(): other = lax.ppermute(own, 'core', [(0, 1), (1, 0)])]
    scatter-add x4 -> x0, other arithmetic: 77.2 us -> none  [the longest x2 38.7 us: level_pass(): gathered.at[:, asked_cells.reshape(-1)]]
    pallas_call x0 -> x3, Pallas kernels: none -> 59.4 us  [the longest x2 57.6 us: level_partial(): pl.pallas_call(functools.partial(level_kernel, scale=scale), grid=(16,),...]
    gather x4 -> x0, local copies, waits for them, and re-layouts: 52.2 us -> none  [the longest x2 26.1 us: level_pass(): jnp.take(moments, first_cells.reshape(-1), axis=1)]
    all_to_all x6 -> x7, starting transfers between devices: 86.5 us -> 46.7 us  [the longest x2 13.4 us: summed_over_parts(): pieces = lax.all_to_all(pieces, ('x', 'comp'), 0, 0, tiled=True)]
    reshape x16, local copies, waits for them, and re-layouts: 46.3 us -> 14.6 us  [the longest x1 6.79 us: slot_lists(): far = gathered[:, 96:].reshape(4, 32, 2, 2, classes, 4, CAP)]
    all_to_all x0 -> x1, blocking collectives: none -> 22.9 us  [spread(): return lax.all_to_all(copies, axis, 0, 0, tiled=True)]
  transfers between devices with their start and end apart: 9 -> 11, of which waited for: 6 -> 5; matrix products, arithmetic and copies ran while one was open for 36% -> 14% of each run, Pallas kernels for 0% -> 24%
where the time goes in v1:
time: 251 us; the launch traced here: 247 us
  Pallas kernels  59.4 us (24%)
  starting transfers between devices  52.9 us (21%)
  waiting for transfers between devices  43.6 us (17%)
  blocking collectives  35.9 us (14%)
  local copies, waits for them, and re-layouts  34 us (14%)
  between operations  14.4 us (6%)
  other arithmetic  6.37 us (3%)
    pallas_call x2, Pallas kernels, level_partial(): pl.pallas_call(functools.partial(level_kernel, scale=scale), grid=(16,),...  57.6 us
    all_to_all x1, blocking collectives, spread(): return lax.all_to_all(copies, axis, 0, 0, tiled=True)  22.9 us
    all_to_all x2, waiting for transfers between devices, summed_over_parts(): pieces = lax.all_to_all(pieces, ('x', 'comp'), 0, 0, tiled=True)  15.5 us
    all_to_all x2, starting transfers between devices, summed_over_parts(): pieces = lax.all_to_all(pieces, ('x', 'comp'), 0, 0, tiled=True)  13.4 us
    all_gather x1, blocking collectives, slot_lists(): lax.all_gather(jnp.concatenate([near.reshape(-1, 128), far.reshape(-1, 12...  13 us
    all_to_all x3, waiting for transfers between devices, spread(): return lax.all_to_all(copies, axis, 0, 0, tiled=True)  13 us
    all_to_all x3, starting transfers between devices, spread(): return lax.all_to_all(copies, axis, 0, 0, tiled=True)  12.6 us
    all_to_all x1, starting transfers between devices, slot_lists(): far = lax.all_to_all(far, ('zh', 'zl', 'core'), 0, 0, tiled=True)  12 us
  transfers between devices with their start and end apart: 11, of which 5 were waited for; matrix products, arithmetic and copies ran while one was open for 14% of the time, Pallas kernels for 24%

profile of v1, /device:TPU:6, one launch (start us, length us, event | category | flops | bytes accessed | tf_op | source)
XLA Modules:
  0.0 246.6 jit_solution(7690780185763388147)
XLA Ops:
  9.0 1.9 collective-permute-start.1
  13.2 8.6 %all-to-all-start.2 = ((s32[4,16,192]{2,1,0:T(8,128)}), s32[4,16,192]{2,1,0:T(8,128)S(1)}, u32[]{:S(2)}, u32[]{:S(2)}) async-start(s32[4,16,192]{2,1,0:T(8,128)} %bitcast.57), calls=%async_computation.2 | async-start | bytes 131072 | tf_op jit(solution)/shard_map/all_to_all | solution.py:158
  25.4 12.0 %all-to-all-start.3 = ((s32[32,3,128]{2,1,0:T(4,128)}), s32[32,3,128]{2,1,0:T(4,128)S(1)}, u32[]{:S(2)}, u32[]{:S(2)}) async-start(s32[32,3,128]{2,1,0:T(4,128)} %copy.65), calls=%async_computation.3 | async-start | bytes 131072 | tf_op jit(solution)/shard_map/all_to_all | solution.py:161
  37.5 1.8 upward.1
  40.0 11.8 %all-to-all-done.3 = s32[32,3,128]{2,1,0:T(4,128)S(1)} async-done(((s32[32,3,128]{2,1,0:T(4,128)}), s32[32,3,128]{2,1,0:T(4,128)S(1)}, u32[]{:S(2)}, u32[]{:S(2)}) %all-to-all-start.3) | async-done | bytes 49184 | tf_op jit(solution)/shard_map/all_to_all | solution.py:161
  52.5 3.3 %all-to-all-start.5 = ((bf16[4,72,128]{2,1,0:T(8,128)(2,1)}), bf16[4,72,128]{2,1,0:T(8,128)(2,1)S(1)}, u32[]{:S(2)}, u32[]{:S(2)}) async-start(bf16[4,72,128]{2,1,0:T(8,128)(2,1)} %broadcast_in_dim.56), calls=%async_computation.5 | async-start | bytes 147456 | tf_op jit(solution)/shard_map/all_to_all | solution.py:107
  55.8 13.0 %all-to-all-done.5 = bf16[4,72,128]{2,1,0:T(8,128)(2,1)S(1)} async-done(((bf16[4,72,128]{2,1,0:T(8,128)(2,1)}), bf16[4,72,128]{2,1,0:T(8,128)(2,1)S(1)}, u32[]{:S(2)}, u32[]{:S(2)}) %all-to-all-start.5) | async-done | bytes 73760 | tf_op jit(solution)/shard_map/all_to_all | solution.py:107
  68.8 22.9 %all_to_all.40 = bf16[4,72,512]{2,1,0:T(8,128)(2,1)S(1)} all-to-all(bf16[4,72,512]{2,1,0:T(8,128)(2,1)S(1)} %broadcast_in_dim.48), channel_id=1, replica_groups=mesh['x'=4,'zh'=4,'zl'=4,'core'=2,'comp'=4] {'zh'}, dimensions={0} | all-to-all | bytes 589824 | tf_op jit(solution)/shard_map/all_to_all | solution.py:107
  92.8 4.3 %all-to-all-start.1 = ((bf16[4,4,72,512]{3,2,1,0:T(8,128)(2,1)}), bf16[4,4,72,512]{3,2,1,0:T(8,128)(2,1)}, u32[]{:S(2)}, u32[]{:S(2)}) async-start(bf16[4,4,72,512]{3,2,1,0:T(8,128)(2,1)} %broadcast_in_dim.49), calls=%async_computation.1 | async-start | bytes 2359296 | tf_op jit(solution)/shard_map/all_to_all | solution.py:107
  98.0 13.0 %all-gather = s32[768,128]{1,0:T(8,128)S(1)} all-gather(s32[192,128]{1,0:T(8,128)S(1)} %pad_add_fusion.1), channel_id=2, replica_groups=mesh['x'=4,'zh'=4,'zl'=4,'core'=2,'comp'=4] {'comp'}, dimensions={0}, use_global_device_ids=true | all-gather | bytes 491520 | tf_op jit(solution)/shard_map/all_gather | solution.py:162
  111.1 6.8 %reshape.90 = s32[4,32,2,2,4,4,6]{6,5,4,3,2,1,0:T(4,128)} reshape(s32[4,96,128]{2,1,0:T(8,128)S(1)} %get-tuple-element.11) | data formatting | bytes 393216 | tf_op jit(solution)/shard_map/reshape | solution.py:166
  117.8 4.7 %slice_bitcast_fusion = (s32[2,4,4,4,32,6]{5,3,2,0,4,1:T(4,128)S(1)}, s32[2,32,6,4,4,4]{2,5,4,0,1,3:T(4,128)}) fusion(s32[4,32,2,2,4,4,6]{6,5,4,3,2,1,0:T(4,128)} %reshape.90), kind=kLoop, calls=%fused_computation.1 | loop fusion | bytes 393216 | tf_op jit(solution)/shard_map/transpose | solution.py:170
  123.8 1.6 reshape.93
  126.3 5.0 %all-to-all-start.6 = ((bf16[4,4,72,128]{3,2,1,0:T(8,128)(2,1)}), bf16[4,4,72,128]{3,2,1,0:T(8,128)(2,1)S(1)}, u32[]{:S(2)}, u32[]{:S(2)}) async-start(bf16[4,4,72,128]{3,2,1,0:T(8,128)(2,1)} %broadcast_in_dim.57), calls=%async_computation.6 | async-start | bytes 589824 | tf_op jit(solution)/shard_map/all_to_all | solution.py:107
  133.1 2.2 reshape.89
  136.7 1.9 collective-permute-start
  140.8 2.4 collective-permute-start.2
  143.2 1.6 all-gather.3.cloned.1.call-done
  144.9 2.1 dynamic-slice_bitcast_fusion
  151.7 23.0 %level.3 = bf16[4,288,128]{2,1,0:T(8,128)(2,1)} custom-call(s32[1]{0:T(128)} %bitcast.core_ref, bf16[16,72,128]{2,1,0:T(8,128)(2,1)} %bitcast.64, bf16[16,72,128]{2,1,0:T(8,128)(2,1)} %copy-done.4, s32[16,2,8,128]{3,2,1,0:T(8,128)} %bitcast.71, s32[128,192]{1,0:T(8,128)} %get-tuple-element.12.dst_ref, bf16[288,2304]{1,0:T(8,128)(2,1)} %pad_maximum_fusion.ops_ref), custom_call_target="tpu_custom_call" | custom-call | flops 3000000000 | bytes 6000000 | tf_op jit(solution)/shard_map/level/pallas_call | solution.py:122
  174.7 6.2 %all-to-all-start.7 = ((bf16[16,72,128]{2,1,0:T(8,128)(2,1)}), bf16[16,72,128]{2,1,0:T(8,128)(2,1)S(1)}, u32[]{:S(2)}, u32[]{:S(2)}) async-start(bf16[16,72,128]{2,1,0:T(8,128)(2,1)} %bitcast.65), calls=%async_computation.7 | async-start | bytes 589824 | tf_op jit(solution)/shard_map/all_to_all | solution.py:148
  180.9 34.6 %level.2 = bf16[4,288,512]{2,1,0:T(8,128)(2,1)} custom-call(s32[1]{0:T(128)} %bitcast.core_ref, bf16[16,72,512]{2,1,0:T(8,128)(2,1)} %bitcast.1.own_ref, bf16[16,72,512]{2,1,0:T(8,128)(2,1)} %collective-permute-done.other_ref, s32[16,2,8,128]{3,2,1,0:T(8,128)} %bitcast.70, s32[128,192]{1,0:T(8,128)} %get-tuple-element.13.dst_ref, ...), custom_call_target="tpu_custom_call" | custom-call | flops 3000000000 | bytes 6000000 | tf_op jit(solution)/shard_map/level/pallas_call | solution.py:122
  215.5 7.2 %all-to-all-start.4 = ((bf16[16,72,512]{2,1,0:T(8,128)(2,1)}), bf16[16,72,512]{2,1,0:T(8,128)(2,1)S(1)}, u32[]{:S(2)}, u32[]{:S(2)}) async-start(bf16[16,72,512]{2,1,0:T(8,128)(2,1)} %bitcast.62), calls=%async_computation.4 | async-start | bytes 2359296 | tf_op jit(solution)/shard_map/all_to_all | solution.py:148
  223.4 15.5 %all-to-all-done.4 = bf16[16,72,512]{2,1,0:T(8,128)(2,1)S(1)} async-done(((bf16[16,72,512]{2,1,0:T(8,128)(2,1)}), bf16[16,72,512]{2,1,0:T(8,128)(2,1)S(1)}, u32[]{:S(2)}, u32[]{:S(2)}) %all-to-all-start.4) | async-done | bytes 1179680 | tf_op jit(solution)/shard_map/all_to_all | solution.py:148
  (78 shorter events, 24.6 us)
Async XLA Ops:
  9.0 15.3 %collective-permute-start.1 = (f32[4,289]{0,1:T(8,128)S(1)}, f32[4,289]{0,1:T(8,128)S(1)}, u32[]{:S(2)}, u32[]{:S(2)}) collective-permute-start(f32[4,289]{0,1:T(8,128)S(1)} %pad_maximum_fusion.1), channel_id=1, source_target_pairs={{0,4},{4,8},{8,12},{12,16},{16,20},{20,24},{24,28},{28,32},{32,36}... | collective-permute-start | bytes 13880 | tf_op jit(solution)/shard_map/ppermute | solution.py:44
  13.2 11.1 %copy-start.2 = (bf16[288,512]{1,0:T(8,128)(2,1)S(1)}, bf16[288,512]{1,0:T(8,128)(2,1)}, u32[]{:S(2)}) copy-start(bf16[288,512]{1,0:T(8,128)(2,1)} %param.6) | copy-start | bytes 884740
  13.2 12.2 %all-to-all-start.2 = ((s32[4,16,192]{2,1,0:T(8,128)}), s32[4,16,192]{2,1,0:T(8,128)S(1)}, u32[]{:S(2)}, u32[]{:S(2)}) async-start(s32[4,16,192]{2,1,0:T(8,128)} %bitcast.57), calls=%async_computation.2 | async-start | bytes 131072 | tf_op jit(solution)/shard_map/all_to_all | solution.py:158
  22.4 15.2 %copy-start = (bf16[8,288,288]{2,1,0:T(8,128)(2,1)S(1)}, bf16[8,288,288]{2,1,0:T(8,128)(2,1)}, u32[]{:S(2)}) copy-start(bf16[8,288,288]{2,1,0:T(8,128)(2,1)} %shifts_ref.1) | copy-start | bytes 3981316
  25.4 26.4 %all-to-all-start.3 = ((s32[32,3,128]{2,1,0:T(4,128)}), s32[32,3,128]{2,1,0:T(4,128)S(1)}, u32[]{:S(2)}, u32[]{:S(2)}) async-start(s32[32,3,128]{2,1,0:T(4,128)} %copy.65), calls=%async_computation.3 | async-start | bytes 131072 | tf_op jit(solution)/shard_map/all_to_all | solution.py:161
  52.5 16.3 %all-to-all-start.5 = ((bf16[4,72,128]{2,1,0:T(8,128)(2,1)}), bf16[4,72,128]{2,1,0:T(8,128)(2,1)S(1)}, u32[]{:S(2)}, u32[]{:S(2)}) async-start(bf16[4,72,128]{2,1,0:T(8,128)(2,1)} %broadcast_in_dim.56), calls=%async_computation.5 | async-start | bytes 147456 | tf_op jit(solution)/shard_map/all_to_all | solution.py:107
  92.8 32.7 %all-to-all-start.1 = ((bf16[4,4,72,512]{3,2,1,0:T(8,128)(2,1)}), bf16[4,4,72,512]{3,2,1,0:T(8,128)(2,1)}, u32[]{:S(2)}, u32[]{:S(2)}) async-start(bf16[4,4,72,512]{3,2,1,0:T(8,128)(2,1)} %broadcast_in_dim.49), calls=%async_computation.1 | async-start | bytes 2359296 | tf_op jit(solution)/shard_map/all_to_all | solution.py:107
  97.1 47.8 %all-gather.3.cloned.1.call-start = ((), (), s32[]{:S(2)}) async-start(), calls=%async_computation.8 | async-start | bytes 4423680 | tf_op jit(solution)/shard_map/all_gather | solution.py:181
  125.4 6.1 %copy-start.1 = (s32[2,32,6,4,4,4]{2,5,4,0,1,3:T(4,128)S(1)}, s32[2,32,6,4,4,4]{2,5,4,0,1,3:T(4,128)}, u32[]{:S(2)}) copy-start(s32[2,32,6,4,4,4]{2,5,4,0,1,3:T(4,128)} %get-tuple-element.9) | copy-start | bytes 294916
  126.3 14.5 %all-to-all-start.6 = ((bf16[4,4,72,128]{3,2,1,0:T(8,128)(2,1)}), bf16[4,4,72,128]{3,2,1,0:T(8,128)(2,1)S(1)}, u32[]{:S(2)}, u32[]{:S(2)}) async-start(bf16[4,4,72,128]{3,2,1,0:T(8,128)(2,1)} %broadcast_in_dim.57), calls=%async_computation.6 | async-start | bytes 589824 | tf_op jit(solution)/shard_map/all_to_all | solution.py:107
  136.7 44.2 %collective-permute-start = (bf16[16,72,512]{2,1,0:T(8,128)(2,1)}, bf16[16,72,512]{2,1,0:T(8,128)(2,1)}, u32[]{:S(2)}, u32[]{:S(2)}) collective-permute-start(bf16[16,72,512]{2,1,0:T(8,128)(2,1)} %bitcast.1.own_ref), channel_id=1, source_target_pairs={{0,4},{4,0},{1,5},{5,1},{2,6},{6,2},{3,7},{7,3},{8,12},{12,8},{9,1... | collective-permute-start | bytes 3538952 | tf_op jit(solution)/shard_map/ppermute | solution.py:111
  140.8 6.9 %copy-start.3 = (bf16[4,4,72,128]{3,2,1,0:T(8,128)(2,1)}, bf16[4,4,72,128]{3,2,1,0:T(8,128)(2,1)S(1)}, u32[]{:S(2)}) copy-start(bf16[4,4,72,128]{3,2,1,0:T(8,128)(2,1)S(1)} %all-to-all-done.6) | copy-start | bytes 884740
  140.8 10.1 %collective-permute-start.2 = (bf16[16,72,128]{2,1,0:T(8,128)(2,1)S(1)}, bf16[16,72,128]{2,1,0:T(8,128)(2,1)S(1)}, u32[]{:S(2)}, u32[]{:S(2)}) collective-permute-start(bf16[16,72,128]{2,1,0:T(8,128)(2,1)S(1)} %bitcast.63), channel_id=1, source_target_pairs={{0,4},{4,0},{1,5},{5,1},{2,6},{6,2},{3,7},{7,3},{8,12},{12,8},{9,1... | collective-permute-start | bytes 884744 | tf_op jit(solution)/shard_map/ppermute | solution.py:111
  150.9 0.7 copy-start.4
  174.7 40.9 %all-to-all-start.7 = ((bf16[16,72,128]{2,1,0:T(8,128)(2,1)}), bf16[16,72,128]{2,1,0:T(8,128)(2,1)S(1)}, u32[]{:S(2)}, u32[]{:S(2)}) async-start(bf16[16,72,128]{2,1,0:T(8,128)(2,1)} %bitcast.65), calls=%async_computation.7 | async-start | bytes 589824 | tf_op jit(solution)/shard_map/all_to_all | solution.py:148
  215.5 23.4 %all-to-all-start.4 = ((bf16[16,72,512]{2,1,0:T(8,128)(2,1)}), bf16[16,72,512]{2,1,0:T(8,128)(2,1)S(1)}, u32[]{:S(2)}, u32[]{:S(2)}) async-start(bf16[16,72,512]{2,1,0:T(8,128)(2,1)} %bitcast.62), calls=%async_computation.4 | async-start | bytes 2359296 | tf_op jit(solution)/shard_map/all_to_all | solution.py:148
Sparse Core Ops, SparseCore 0:
  100.0 44.7 all-gather.2

commit v2 on v1

v2 whole, which is shorter than its diff:
```python
import functools

import jax
import jax.numpy as jnp
from jax import lax
from jax.experimental import pallas as pl
from jax.experimental.pallas import tpu as pltpu
from jax.sharding import Mesh
from jax.sharding import PartitionSpec as P

CAP = 6
CODE_OFFSET = 256
NO_CELL = 1024
CELLS = ("x", "zh", "zl", "core")
BF16 = jnp.bfloat16
F32 = jnp.float32


def upward_kernel(moments_ref, slot_ref, shifts_ref, out_ref):
    octants, width, _ = shifts_ref.shape
    coarse = out_ref.shape[1]
    spots = octants * coarse
    rows = lax.broadcasted_iota(jnp.int32, (spots, slot_ref.shape[1]), 0)
    hot = (rows == slot_ref[0:1, :]).astype(BF16)
    placed = lax.dot_general(
        moments_ref[...], hot, (((1,), (1,)), ((), ())), preferred_element_type=F32
    ).astype(BF16)
    total = jnp.zeros((width, coarse), F32)
    for octant in range(octants):
        part = placed[:, octant * coarse : (octant + 1) * coarse]
        total = total + jnp.dot(shifts_ref[octant], part, preferred_element_type=F32)
    out_ref[...] = total.astype(BF16)


def edge_from_before(moments, child_links):
    coarse = moments.shape[1] // 4
    group = lax.axis_index(CELLS)
    devices = lax.axis_size(CELLS)
    parent = child_links[0] - group * coarse
    octant = child_links[1]
    inside = parent < coarse
    slot = jnp.where(inside, octant * coarse + parent, -1)
    code = jnp.where(inside, -1, octant)[-4:].astype(F32)
    edge = jnp.concatenate([moments[:, -4:].T.astype(F32), code[:, None]], axis=1)
    return slot, lax.ppermute(edge, CELLS, [(i, i + 1) for i in range(devices - 1)])


def upward(moments, slot, edge, shifts_up):
    width, fine = moments.shape
    coarse = fine // 4
    edge_code = edge[:, width].astype(jnp.int32)
    edge_slot = jnp.where(edge_code >= 0, edge_code * coarse, -1)
    edge_moments = edge[:, :width].T.astype(BF16)
    pad = 124
    slots = jnp.concatenate([slot, edge_slot, jnp.full((pad,), -1, jnp.int32)])
    extended = jnp.concatenate([moments, edge_moments, jnp.zeros((width, pad), BF16)], axis=1)
    return pl.pallas_call(
        upward_kernel,
        out_shape=jax.ShapeDtypeStruct((width, coarse), BF16),
        compiler_params=pltpu.CompilerParams(vmem_limit_bytes=48 * 1024 * 1024),
        cost_estimate=pl.CostEstimate(flops=8 * 10**8, bytes_accessed=2 * 10**6, transcendentals=0),
        name="upward",
    )(extended, slots.reshape(1, -1), shifts_up)


def one_hot(row, cells):
    count = row.shape[1]
    part = min(cells, 256)
    place = lax.broadcasted_iota(jnp.int32, (part, count), 0).astype(F32).astype(BF16)
    ones, zeros = jnp.ones((part, count), BF16), jnp.zeros((part, count), BF16)
    tiles = []
    for first in range(0, cells, part):
        wanted = jnp.broadcast_to((row - first).astype(F32), (part, count)).astype(BF16)
        tiles.append(jnp.where(place == wanted, ones, zeros))
    return tiles[0] if len(tiles) == 1 else jnp.concatenate(tiles, axis=0)


def regrouped(arrays, lane_bits):
    arrays = [arrays[-j % 16] for j in range(16)]
    for b in range(4):
        arrays = [
            jnp.where(lane_bits[b], arrays[(j - (1 << b)) % 16], arrays[j]) for j in range(16)
        ]
    return arrays


def level_kernel(*refs, pieces, scale):
    place_ref, order_ref = refs[:2]
    blocks = refs[2 : 2 + 2 * pieces]
    src_ref, dst_ref, ops_ref, out_ref, picked_ref, group_ref, sums_ref = refs[2 + 2 * pieces :]
    height, cells = ops_ref.shape[0] // 32, blocks[0].shape[2]
    core, me = place_ref[0], place_ref[1]

    first = 0
    for own_ref, other_ref in zip(blocks[0::2], blocks[1::2]):

        def pick(i, carry, own_ref=own_ref, other_ref=other_ref, first=first):
            z = order_ref[first + i]
            for block_ref, side in ((own_ref, core), (other_ref, 1 - core)):
                h = z * 2 + side
                block = block_ref[i]
                held = block.shape[0]
                for part in range(4):
                    row = src_ref[pl.ds(h, 1), part * 256 : (part + 1) * 256]
                    picked = jnp.dot(block, one_hot(row, cells), preferred_element_type=F32)
                    picked = picked.astype(BF16)
                    picked_ref[h, 2 * part, 0:held] = picked[:, 0:128]
                    picked_ref[h, 2 * part + 1, 0:held] = picked[:, 128:256]
            return carry

        lax.fori_loop(0, own_ref.shape[0], pick, 0)
        first += own_ref.shape[0]

    lane = lax.broadcasted_iota(jnp.int32, (16, 128), 1) // 8
    lane_bits = [(lane >> b) & 1 == 1 for b in range(4)]
    padded = group_ref.shape[1]

    def add_up(q, carry):
        for half in range(2):
            for top in range(0, padded, 16):
                rows = slice(top, top + 16)
                arrays = [picked_ref[half * 16 + j, q, rows, :] for j in range(16)]
                for j, array in enumerate(regrouped(arrays, lane_bits)):
                    group_ref[j, rows, half * 128 : (half + 1) * 128] = array
        for half in range(2):
            lists = dst_ref[pl.ds(pl.multiple_of(q * 16 + half * 8, 8), 8), :]
            for target in range(2):
                for couple in range(2):
                    sums = []
                    for j in (target * 4 + couple * 2, target * 4 + couple * 2 + 1):
                        sums.append(
                            lax.dot_general(
                                group_ref[half * 8 + j, 0:height],
                                one_hot(lists[j : j + 1, :], cells),
                                (((1,), (1,)), ((), ())),
                                preferred_element_type=F32,
                            )
                        )
                    distance = (me + 4 - q % 4) % 4
                    start = (distance * 2 + q // 4) * 2 + couple
                    start = pl.multiple_of(start * (2 * height), 2 * height)
                    sums_ref[half * 2 + target, pl.ds(start, 2 * height), :] = jnp.concatenate(
                        sums, axis=0
                    ).astype(BF16)
        return carry

    lax.fori_loop(0, 8, add_up, 0)
    operators = ops_ref[...].T
    for target in range(4):
        total = jnp.dot(operators, sums_ref[target], preferred_element_type=F32)
        out_ref[target] = (total * scale).astype(BF16)


def own_rows(moments):
    height = moments.shape[0] // 4
    return lax.dynamic_slice_in_dim(moments, lax.axis_index("comp") * height, height, 0)


def other_core(array):
    return lax.ppermute(array, "core", [(0, 1), (1, 0)])


def spread_to(block, axis):
    copies = jnp.broadcast_to(block[None], (4,) + block.shape)
    return lax.all_to_all(copies, axis, 0, 0, tiled=True)


def spread_at_once(block):
    copies = jnp.broadcast_to(block[None], (16,) + block.shape)
    return lax.all_to_all(copies, ("zh", "zl"), 0, 0, tiled=True)


def level_partial(pieces, order, src, dst, operators, scale):
    blocks = [block for own, other in pieces for block in (own, other)]
    cells = blocks[0].shape[2]
    width = operators.shape[1]
    height = width // 4
    padded = -(-height // 16) * 16
    smem = pl.BlockSpec(memory_space=pltpu.SMEM)
    vmem = pl.BlockSpec(memory_space=pltpu.VMEM)
    return pl.pallas_call(
        functools.partial(level_kernel, pieces=len(pieces), scale=scale),
        in_specs=[smem, smem] + [vmem] * (len(blocks) + 3),
        out_specs=vmem,
        out_shape=jax.ShapeDtypeStruct((4, width, cells), BF16),
        scratch_shapes=[
            pltpu.VMEM((32, 8, padded, 128), BF16),
            pltpu.VMEM((16, padded, 256), BF16),
            pltpu.VMEM((4, 32 * height, cells), BF16),
        ],
        compiler_params=pltpu.CompilerParams(vmem_limit_bytes=48 * 1024 * 1024),
        cost_estimate=pl.CostEstimate(
            flops=5 * 10**7 * cells, bytes_accessed=6 * 10**6, transcendentals=0
        ),
        name="level",
    )(jnp.stack([lax.axis_index("core"), lax.axis_index("comp")]), order, *blocks, src, dst, operators)


def summed_over_parts(partial):
    groups, width, cells = partial.shape
    pieces = partial.reshape(groups * 4, width // 4, cells)
    pieces = lax.all_to_all(pieces, ("x", "comp"), 0, 0, tiled=True)
    return jnp.sum(pieces.astype(F32), axis=0)


def turned(rows):
    return pltpu.roll(rows, 0, 1, stride=8, stride_axis=0)


def crossed(rows, lane_bits):
    rows = jnp.concatenate([rows[0:1]] + [rows[j : j + 1] for j in range(15, 0, -1)], axis=0)
    for b in range(4):
        rows = jnp.where(lane_bits[b], pltpu.roll(rows, 1 << b, 0), rows)
    return rows


def lists_kernel(x_ref, near_ref, far_ref, *out_refs):
    lane = lax.broadcasted_iota(jnp.int32, (16, 128), 1) // 8
    lane_bits = [(lane >> b) & 1 == 1 for b in range(4)]

    def cells_of(codes):
        return codes.astype(F32).astype(jnp.int32) + CODE_OFFSET

    for part in range(4):
        for half in range(2):
            near_lists = [cells_of(near_ref[part, (x_ref[0] + 4 - g) % 4, half]) for g in range(4)]
            for level in range(2):
                src_ref, dst_ref = out_refs[2 * level : 2 * level + 2]
                lanes = slice(half * 128, (half + 1) * 128)
                hs = slice(half * 16, (half + 1) * 16)

                def near(value):
                    kind = (level * 2 + value) * 4
                    return jnp.concatenate(
                        [lists[kind : kind + 4] for lists in near_lists], axis=0
                    )

                def far(value):
                    return cells_of(far_ref[part, level * 2 + value, hs, :])

                src_ref[hs, part * 128 : (part + 1) * 128] = crossed(
                    turned(near(0)), lane_bits
                )
                dst_ref[part * 16 : (part + 1) * 16, lanes] = turned(near(1))
                src_ref[hs, (part + 4) * 128 : (part + 5) * 128] = turned(far(0))
                dst_ref[(part + 4) * 16 : (part + 5) * 16, lanes] = crossed(
                    turned(far(1)), lane_bits
                )


def slot_messages(fine_pairs, coarse_pairs):
    both = jnp.stack([fine_pairs, coarse_pairs])
    first, second, alive = both[:, 0], both[:, 1], both[:, 2] == 1
    classes = first.shape[1]

    def slots(source, target):
        lists = jnp.stack([jnp.where(alive, source - CODE_OFFSET, NO_CELL), target - CODE_OFFSET], 1)
        lists = lists.astype(BF16).reshape(2, 2, classes, 4, 32, CAP)
        return jnp.pad(lists, [(0, 0)] * 5 + [(0, 8 - CAP)], constant_values=NO_CELL)

    near = slots(second, first).reshape(2, 2, classes, 4, 2, 128)
    near = near.transpose(3, 4, 0, 1, 2, 5).reshape(4, 8 * classes, 128)
    far = slots(first, second).transpose(4, 0, 1, 3, 2, 5).reshape(4, 4, 8, 128)
    far = jnp.concatenate([far[:, j] for j in range(4)], axis=-1)
    return near, far


def passed(array, axis, distance):
    if distance == 0:
        return array
    count = lax.axis_size(axis)
    return lax.ppermute(array, axis, [(i, (i + distance) % count) for i in range(count)])


def parts_for(array, name, axis):
    me = lax.axis_index(name)
    return [
        lax.dynamic_index_in_dim(array, (me + distance) % 4, axis, keepdims=False)
        for distance in range(4)
    ]


def exchanged(parts, name):
    return jnp.stack([passed(part, name, distance) for distance, part in enumerate(parts)])


def lists_from_chip_and_comp(near, blocks):
    rows = blocks[:, 72:].reshape(4, 4, 2, 4, -1)
    rows = lax.dynamic_slice_in_dim(rows, lax.axis_index("zl") * 128, 128, 4)
    rows = rows.transpose(2, 0, 1, 3, 4).reshape(2, 64, 128)
    near = jnp.broadcast_to(near.reshape(1, 128, 128), (2, 128, 128))
    rows = jnp.concatenate([rows, near], axis=1)
    rows = jnp.broadcast_to(rows[:, None], (2, 4, 192, 128)).reshape(8, 192, 128)
    rows = lax.all_to_all(rows, ("core", "comp"), 0, 0, tiled=True).reshape(2, 4, 192, 128)
    near = lax.dynamic_index_in_dim(rows[:, :, 64:], lax.axis_index("core"), 0, keepdims=False)
    far = rows[:, :, :64].reshape(2, 4, 4, 4, 4, 128).transpose(1, 4, 3, 2, 0, 5)
    return near.reshape(4, 4, 2, 16, 128), far.reshape(4, 4, 32, 128)


def slot_lists(near, far):
    vmem = pl.BlockSpec(memory_space=pltpu.VMEM)
    return pl.pallas_call(
        lists_kernel,
        in_specs=[pl.BlockSpec(memory_space=pltpu.SMEM), vmem, vmem],
        out_specs=[vmem] * 4,
        out_shape=[
            jax.ShapeDtypeStruct((32, 1024), jnp.int32),
            jax.ShapeDtypeStruct((128, 256), jnp.int32),
        ]
        * 2,
        name="lists",
    )(lax.axis_index("x").reshape(1), near, far)


def operator_parts(translations):
    classes, width, _ = translations.shape
    both = jnp.stack([translations, translations.swapaxes(1, 2)])
    return parts_for(both.reshape(2, classes, 4, width // 4, width), "comp", 2)


def per_device(fine_moments, translations, shifts_up, fine_pairs, coarse_pairs, child_links):
    near, far = slot_messages(fine_pairs, coarse_pairs)
    rows = own_rows(fine_moments)
    copies = jnp.broadcast_to(rows[None], (4,) + rows.shape)
    four = lax.all_to_all(jnp.concatenate([copies, far], axis=1), "zh", 0, 0, tiled=True)
    slot, edge = edge_from_before(fine_moments, child_links)
    near, operators = parts_for(near, "x", 0), operator_parts(translations)
    four, edge, near, operators = lax.optimization_barrier((four, edge, near, operators))
    fine = spread_to(four, "zl").reshape((16,) + four.shape[1:])
    near = exchanged(near, "x")
    operators = exchanged(operators, "comp").reshape(-1, fine_moments.shape[0])
    coarse_moments = upward(fine_moments, slot, edge, shifts_up)
    near, operators, coarse_rows, fine = lax.optimization_barrier(
        (near, operators, own_rows(coarse_moments), fine)
    )
    fine_other = other_core(fine)
    fine_src, fine_dst, coarse_src, coarse_dst = slot_lists(*lists_from_chip_and_comp(near, fine))
    coarse_rows, fine_src = lax.optimization_barrier((coarse_rows, fine_src))
    place = jnp.arange(16, dtype=jnp.int32)
    order = place % 4 * 4 + place // 4
    fine_partial = level_partial([(fine, fine_other)], order, fine_src, fine_dst, operators, 1.0)

    coarse = spread_at_once(coarse_rows)
    coarse, fine_partial = lax.optimization_barrier((coarse, fine_partial))
    other = other_core(coarse)
    coarse_partial = level_partial(
        [(coarse, other)], place, coarse_src, coarse_dst, operators, 0.5
    )
    fine_locals = summed_over_parts(fine_partial)
    coarse_partial, fine_locals = lax.optimization_barrier((coarse_partial, fine_locals))
    return (fine_locals, coarse_moments, summed_over_parts(coarse_partial))


def solution(mesh):
    split = Mesh(mesh.devices.reshape(4, 4, 4, 2, 4), CELLS + ("comp",))
    return jax.shard_map(
        per_device,
        mesh=split,
        in_specs=(
            P(None, CELLS),
            P("comp", None, None),
            P(),
            P(None, "comp", CELLS),
            P(None, "comp", CELLS),
            P(None, CELLS),
        ),
        out_specs=(P("comp", CELLS), P(None, CELLS), P("comp", CELLS)),
        check_vma=False,
    )
```

time: 251 us -> 174 us (0.69)
  blocking collectives: 35.9 us -> 12.8 us
  Pallas kernels: 59.4 us -> 39.6 us
  local copies, waits for them, and re-layouts: 34 us -> 17.5 us
  between operations: 14.4 us -> 1.24 us
  waiting for transfers between devices: 43.6 us -> 30.8 us
  starting transfers between devices: 52.9 us -> 60.4 us
    pallas_call x2 -> x3, Pallas kernels: 57.6 us -> 37.9 us  [the longest x2 35.9 us: level_partial(): pl.pallas_call(functools.partial(level_kernel, pieces=len(pieces), scale=...]
    ppermute x3 -> x9, starting transfers between devices: 6.24 us -> 25.9 us  [the longest x6 20.2 us: passed(): lax.ppermute(array, axis, [(i, (i + distance) % count) for i in range(cou...]
    ppermute x3 -> x9, waiting for transfers between devices: 0.01 us -> 17 us  [the longest x1 12 us: edge_from_before(): lax.ppermute(edge, CELLS, [(i, i + 1) for i in range(devices - 1)])]
    all_to_all x2 -> x1, waiting for transfers between devices: 15.5 us -> 1.3 us  [summed_over_parts(): pieces = lax.all_to_all(pieces, ('x', 'comp'), 0, 0, tiled=True)]
    reshape x15 -> x3, local copies, waits for them, and re-layouts: 14.6 us -> 1.02 us  [the longest x1 0.49 us: slot_messages(): far = slots(first, second).transpose(4, 0, 1, 3, 2, 5).reshape(4, 4, 8, 128)]
    all_to_all x5 -> x4, waiting for transfers between devices: 25.8 us -> 12.5 us  [the longest x1 8.16 us: lists_from_chip_and_comp(): lax.all_to_all(rows, ('core', 'comp'), 0, 0, tiled=True)]
    all_gather x1 -> x0, blocking collectives: 13 us -> none  [slot_lists(): lax.all_gather(jnp.concatenate([near.reshape(-1, 128), far.reshape(-1, 12...]
    all_to_all x1, blocking collectives: 22.9 us -> 12.8 us  [summed_over_parts(): pieces = lax.all_to_all(pieces, ('x', 'comp'), 0, 0, tiled=True)]
  transfers between devices with their start and end apart: 11 -> 14, of which waited for: 5 -> 6; matrix products, arithmetic and copies ran while one was open for 14% -> 8% of each run, Pallas kernels for 24% -> 23%
where the time goes in v2:
time: 174 us; the launch traced here: 171 us
  starting transfers between devices  60.4 us (35%)
  Pallas kernels  39.6 us (23%)
  waiting for transfers between devices  30.8 us (18%)
  local copies, waits for them, and re-layouts  17.5 us (10%)
  blocking collectives  12.8 us (7%)
  other arithmetic  8.38 us (5%)
    pallas_call x2, Pallas kernels, level_partial(): pl.pallas_call(functools.partial(level_kernel, pieces=len(pieces), scale=...  35.9 us
    ppermute x6, starting transfers between devices, passed(): lax.ppermute(array, axis, [(i, (i + distance) % count) for i in range(cou...  20.2 us
    all_to_all x1, starting transfers between devices, per_device(): lax.all_to_all(jnp.concatenate([copies, far], axis=1), 'zh', 0, 0, tiled=...  15.1 us
    all_to_all x1, blocking collectives, summed_over_parts(): pieces = lax.all_to_all(pieces, ('x', 'comp'), 0, 0, tiled=True)  12.8 us
    ppermute x1, waiting for transfers between devices, edge_from_before(): lax.ppermute(edge, CELLS, [(i, i + 1) for i in range(devices - 1)])  12 us
    all_to_all x1, waiting for transfers between devices, lists_from_chip_and_comp(): lax.all_to_all(rows, ('core', 'comp'), 0, 0, tiled=True)  8.16 us
    all_to_all x1, starting transfers between devices, spread_at_once(): return lax.all_to_all(copies, ('zh', 'zl'), 0, 0, tiled=True)  5.93 us
    all_to_all x1, starting transfers between devices, summed_over_parts(): pieces = lax.all_to_all(pieces, ('x', 'comp'), 0, 0, tiled=True)  5.87 us
  transfers between devices with their start and end apart: 14, of which 6 were waited for; matrix products, arithmetic and copies ran while one was open for 8% of the time, Pallas kernels for 23%

profile of v2, /device:TPU:6, one launch (start us, length us, event | category | flops | bytes accessed | tf_op | source)
XLA Modules:
  0.0 170.7 jit_solution(3525366987899835872)
XLA Ops:
  5.5 15.1 %all-to-all-start = ((bf16[4,80,512]{2,1,0:T(8,128)(2,1)}), bf16[4,80,512]{2,1,0:T(8,128)(2,1)}, u32[]{:S(2)}, u32[]{:S(2)}) async-start(bf16[4,80,512]{2,1,0:T(8,128)(2,1)} %maximum_maximum_fusion.1), calls=%async_computation | async-start | bytes 655360 | tf_op jit(solution)/shard_map/all_to_all | solution.py:325
  20.8 1.9 %collective-permute-start = (f32[4,289]{0,1:T(8,128)S(1)}, f32[4,289]{0,1:T(8,128)}, u32[]{:S(2)}, u32[]{:S(2)}) collective-permute-start(f32[4,289]{0,1:T(8,128)S(1)} %pad_maximum_fusion.1), channel_id=1, source_target_pairs={{0,4},{4,8},{8,12},{12,16},{16,20},{20,24},{24,28},{28,32},{32,36}... | collective-permute-start | bytes 13880 | tf_op jit(solution)/shard_map/ppermute | solution.py:45
  28.3 12.0 %collective-permute-done = f32[4,289]{0,1:T(8,128)} collective-permute-done((f32[4,289]{0,1:T(8,128)S(1)}, f32[4,289]{0,1:T(8,128)}, u32[]{:S(2)}, u32[]{:S(2)}) %collective-permute-start) | collective-permute-done | bytes 4656 | tf_op jit(solution)/shard_map/ppermute | solution.py:45
  40.3 4.3 %all-to-all-done = bf16[4,80,512]{2,1,0:T(8,128)(2,1)} async-done(((bf16[4,80,512]{2,1,0:T(8,128)(2,1)}), bf16[4,80,512]{2,1,0:T(8,128)(2,1)}, u32[]{:S(2)}, u32[]{:S(2)}) %all-to-all-start) | async-done | bytes 327712 | tf_op jit(solution)/shard_map/all_to_all | solution.py:325
  44.6 2.2 %broadcast_in_dim.62 = bf16[4,4,80,512]{3,2,1,0:T(8,128)(2,1)} broadcast(bf16[4,80,512]{2,1,0:T(8,128)(2,1)} %all-to-all-done), dimensions={1,2,3} | broadcast | bytes 1638400 | tf_op jit(solution)/shard_map/broadcast_in_dim | solution.py:164
  46.8 4.1 %all-to-all-start.1 = ((bf16[4,4,80,512]{3,2,1,0:T(8,128)(2,1)}), bf16[4,4,80,512]{3,2,1,0:T(8,128)(2,1)S(1)}, u32[]{:S(2)}, u32[]{:S(2)}) async-start(bf16[4,4,80,512]{3,2,1,0:T(8,128)(2,1)} %broadcast_in_dim.62), calls=%async_computation.1 | async-start | bytes 2621440 | tf_op jit(solution)/shard_map/all_to_all | solution.py:165
  51.0 3.5 %collective-permute-start.4 = (bf16[2,4,72,288]{3,2,1,0:T(8,128)(2,1)}, bf16[2,4,72,288]{3,2,1,0:T(8,128)(2,1)S(1)}, u32[]{:S(2)}, u32[]{:S(2)}) collective-permute-start(bf16[2,4,72,288]{3,2,1,0:T(8,128)(2,1)} %get-tuple-element.32), channel_id=1, source_target_pairs={{0,1},{1,2},{2,3},{3,0},{4,5},{5,6},{6,7},{7,4},{8,9},{9,10},{10,1... | collective-permute-start | bytes 995336 | tf_op jit(solution)/shard_map/ppermute | solution.py:272
  54.5 4.8 %collective-permute-start.5 = (bf16[2,4,72,288]{3,2,1,0:T(8,128)(2,1)}, bf16[2,4,72,288]{3,2,1,0:T(8,128)(2,1)S(1)}, u32[]{:S(2)}, u32[]{:S(2)}) collective-permute-start(bf16[2,4,72,288]{3,2,1,0:T(8,128)(2,1)} %get-tuple-element.33), channel_id=1, source_target_pairs={{0,2},{1,3},{2,0},{3,1},{4,6},{5,7},{6,4},{7,5},{8,10},{9,11},{10,... | collective-permute-start | bytes 995336 | tf_op jit(solution)/shard_map/ppermute | solution.py:272
  59.3 3.3 %collective-permute-start.6 = (bf16[2,4,72,288]{3,2,1,0:T(8,128)(2,1)}, bf16[2,4,72,288]{3,2,1,0:T(8,128)(2,1)S(1)}, u32[]{:S(2)}, u32[]{:S(2)}) collective-permute-start(bf16[2,4,72,288]{3,2,1,0:T(8,128)(2,1)} %get-tuple-element.34), channel_id=1, source_target_pairs={{0,3},{1,0},{2,1},{3,2},{4,7},{5,4},{6,5},{7,6},{8,11},{9,8},{10,9... | collective-permute-start | bytes 995336 | tf_op jit(solution)/shard_map/ppermute | solution.py:272
  62.6 2.4 %collective-permute-start.1 = (bf16[32,128]{1,0:T(8,128)(2,1)S(1)}, bf16[32,128]{1,0:T(8,128)(2,1)S(1)}, u32[]{:S(2)}, u32[]{:S(2)}) collective-permute-start(bf16[32,128]{1,0:T(8,128)(2,1)S(1)} %get-tuple-element.28), channel_id=1, source_target_pairs={{0,128},{128,256},{256,384},{384,0},{1,129},{129,257},{257,385},{3... | collective-permute-start | bytes 24584 | tf_op jit(solution)/shard_map/ppermute | solution.py:272
  64.9 4.3 %collective-permute-start.2 = (bf16[32,128]{1,0:T(8,128)(2,1)S(1)}, bf16[32,128]{1,0:T(8,128)(2,1)S(1)}, u32[]{:S(2)}, u32[]{:S(2)}) collective-permute-start(bf16[32,128]{1,0:T(8,128)(2,1)S(1)} %get-tuple-element.29), channel_id=1, source_target_pairs={{0,256},{128,384},{256,0},{384,128},{1,257},{129,385},{257,1},{385... | collective-permute-start | bytes 24584 | tf_op jit(solution)/shard_map/ppermute | solution.py:272
  73.8 1.9 %collective-permute-start.3 = (bf16[32,128]{1,0:T(8,128)(2,1)S(1)}, bf16[32,128]{1,0:T(8,128)(2,1)S(1)}, u32[]{:S(2)}, u32[]{:S(2)}) collective-permute-start(bf16[32,128]{1,0:T(8,128)(2,1)S(1)} %get-tuple-element.30), channel_id=1, source_target_pairs={{0,384},{128,0},{256,128},{384,256},{1,385},{129,1},{257,129},{385... | collective-permute-start | bytes 24584 | tf_op jit(solution)/shard_map/ppermute | solution.py:272
  77.1 3.5 %collective-permute-done.3 = bf16[32,128]{1,0:T(8,128)(2,1)S(1)} collective-permute-done((bf16[32,128]{1,0:T(8,128)(2,1)S(1)}, bf16[32,128]{1,0:T(8,128)(2,1)S(1)}, u32[]{:S(2)}, u32[]{:S(2)}) %collective-permute-start.3) | collective-permute-done | bytes 8224 | tf_op jit(solution)/shard_map/ppermute | solution.py:272
  81.0 1.9 %collective-permute-start.7 = (bf16[16,80,512]{2,1,0:T(8,128)(2,1)S(1)}, bf16[16,80,512]{2,1,0:T(8,128)(2,1)}, u32[]{:S(2)}, u32[]{:S(2)}) collective-permute-start(bf16[16,80,512]{2,1,0:T(8,128)(2,1)S(1)} %bitcast.80), channel_id=1, source_target_pairs={{0,4},{4,0},{1,5},{5,1},{2,6},{6,2},{3,7},{7,3},{8,12},{12,8},{9,1... | collective-permute-start | bytes 3932168 | tf_op jit(solution)/shard_map/ppermute | solution.py:160
  83.9 3.5 %all-to-all-start.2 = ((bf16[8,192,128]{2,1,0:T(8,128)(2,1)}), bf16[8,192,128]{2,1,0:T(8,128)(2,1)S(1)}, u32[]{:S(2)}, u32[]{:S(2)}) async-start(bf16[8,192,128]{2,1,0:T(8,128)(2,1)} %bitcast.90), calls=%async_computation.2 | async-start | bytes 786432 | tf_op jit(solution)/shard_map/all_to_all | solution.py:294
  87.5 8.2 %all-to-all-done.2 = bf16[8,192,128]{2,1,0:T(8,128)(2,1)S(1)} async-done(((bf16[8,192,128]{2,1,0:T(8,128)(2,1)}), bf16[8,192,128]{2,1,0:T(8,128)(2,1)S(1)}, u32[]{:S(2)}, u32[]{:S(2)}) %all-to-all-start.2) | async-done | bytes 393248 | tf_op jit(solution)/shard_map/all_to_all | solution.py:294
  97.1 2.0 %lists.1 = (s32[32,1024]{1,0:T(8,128)}, s32[128,256]{1,0:T(8,128)}, s32[32,1024]{1,0:T(8,128)}, s32[128,256]{1,0:T(8,128)}) custom-call(s32[1]{0:T(128)} %bitcast.38.x_ref, bf16[4,4,2,16,128]{4,3,2,1,0:T(8,128)(2,1)} %bitcast.92, bf16[4,4,32,128]{3,2,1,0:T(8,128)(2,1)} %bitcast.91), custom_call_target="tpu_custom_call" | custom-call | tf_op jit(solution)/shard_map/lists/pallas_call | solution.py:302
  99.9 5.9 %all-to-all-start.3 = ((bf16[16,72,128]{2,1,0:T(8,128)(2,1)}), bf16[16,72,128]{2,1,0:T(8,128)(2,1)S(1)}, u32[]{:S(2)}, u32[]{:S(2)}) async-start(bf16[16,72,128]{2,1,0:T(8,128)(2,1)} %broadcast_in_dim.66), calls=%async_computation.3 | async-start | bytes 589824 | tf_op jit(solution)/shard_map/all_to_all | solution.py:170
  107.6 24.3 %level.2 = bf16[4,288,512]{2,1,0:T(8,128)(2,1)S(1)} custom-call(s32[2]{0:T(128)S(1)} %pad_add_fusion.2.refs_0_, s32[16]{0:T(128)S(1)} %fusion.19.refs_1_, bf16[16,80,512]{2,1,0:T(8,128)(2,1)S(1)} %bitcast.82, bf16[16,80,512]{2,1,0:T(8,128)(2,1)} %collective-permute-done.7.refs_3_, s32[32,1024]{1,0:T(8,128)S(1)} %copy-done.4, s32[128,256]{1,0:T(8,128)S(1)} %copy-done.5, ...), custom_call_target="tpu_custom_call" | custom-call | flops 25600000000 | bytes 6000000 | tf_op jit(solution)/shard_map/level/pallas_call | solution.py:181
  133.0 5.9 %all-to-all-start.4 = ((bf16[16,72,512]{2,1,0:T(8,128)(2,1)}), bf16[16,72,512]{2,1,0:T(8,128)(2,1)}, u32[]{:S(2)}, u32[]{:S(2)}) async-start(bf16[16,72,512]{2,1,0:T(8,128)(2,1)} %bitcast.83), calls=%async_computation.4 | async-start | bytes 2359296 | tf_op jit(solution)/shard_map/all_to_all | solution.py:202
  138.8 1.9 %collective-permute-start.8 = (bf16[16,72,128]{2,1,0:T(8,128)(2,1)S(1)}, bf16[16,72,128]{2,1,0:T(8,128)(2,1)S(1)}, u32[]{:S(2)}, u32[]{:S(2)}) collective-permute-start(bf16[16,72,128]{2,1,0:T(8,128)(2,1)S(1)} %all-to-all-done.3.refs_2_), channel_id=1, source_target_pairs={{0,4},{4,0},{1,5},{5,1},{2,6},{6,2},{3,7},{7,3},{8,12},{12,8},{9,1... | collective-permute-start | bytes 884744 | tf_op jit(solution)/shard_map/ppermute | solution.py:160
  142.3 11.6 %level.3 = bf16[4,288,128]{2,1,0:T(8,128)(2,1)S(1)} custom-call(s32[2]{0:T(128)S(1)} %pad_add_fusion.2.refs_0_, s32[16]{0:T(128)S(1)} %iota.5.refs_1_, bf16[16,72,128]{2,1,0:T(8,128)(2,1)S(1)} %all-to-all-done.3.refs_2_, bf16[16,72,128]{2,1,0:T(8,128)(2,1)S(1)} %collective-permute-done.8.refs_3_, s32[32,1024]{1,0:T(8,128)S(1)} %copy-done.2, ...), custom_call_target="tpu_custom_call" | custom-call | flops 6400000000 | bytes 6000000 | tf_op jit(solution)/shard_map/level/pallas_call | solution.py:181
  155.2 2.1 %convert_reduce_fusion = f32[72,512]{1,0:T(8,128)} fusion(bf16[16,72,512]{2,1,0:T(8,128)(2,1)} %all-to-all-done.4), kind=kLoop, calls=%fused_computation.8 | loop fusion | flops 1142784 | bytes 1327104 | tf_op jit(solution)/shard_map/reduce_sum | solution.py:203
  157.3 12.8 %all_to_all.30 = bf16[16,72,128]{2,1,0:T(8,128)(2,1)S(1)} all-to-all(bf16[16,72,128]{2,1,0:T(8,128)(2,1)S(1)} %bitcast.84), channel_id=1, replica_groups=mesh['x'=4,'zh'=4,'zl'=4,'core'=2,'comp'=4] {'x','comp'}, dimensions={0} | all-to-all | bytes 589824 | tf_op jit(solution)/shard_map/all_to_all | solution.py:202
  (90 shorter events, 26.3 us)
Async XLA Ops:
  0.6 4.0 %copy-start.7 = (bf16[288,512]{1,0:T(8,128)(2,1)S(1)}, bf16[288,512]{1,0:T(8,128)(2,1)}, u32[]{:S(2)}) copy-start(bf16[288,512]{1,0:T(8,128)(2,1)} %param.6) | copy-start | bytes 884740
  2.9 17.7 %copy-start.10 = (s32[2,512]{1,0:T(2,128)S(1)}, s32[2,512]{1,0:T(2,128)}, u32[]{:S(2)}) copy-start(s32[2,512]{1,0:T(2,128)} %param.11) | copy-start | bytes 12292
  4.2 18.7 %copy-start.6 = (bf16[4,288,288]{2,1,0:T(8,128)(2,1)S(1)}, bf16[4,288,288]{2,1,0:T(8,128)(2,1)}, u32[]{:S(2)}) copy-start(bf16[4,288,288]{2,1,0:T(8,128)(2,1)} %param.7) | copy-start | bytes 1990660
  5.5 39.1 %all-to-all-start = ((bf16[4,80,512]{2,1,0:T(8,128)(2,1)}), bf16[4,80,512]{2,1,0:T(8,128)(2,1)}, u32[]{:S(2)}, u32[]{:S(2)}) async-start(bf16[4,80,512]{2,1,0:T(8,128)(2,1)} %maximum_maximum_fusion.1), calls=%async_computation | async-start | bytes 655360 | tf_op jit(solution)/shard_map/all_to_all | solution.py:325
  20.8 19.5 %collective-permute-start = (f32[4,289]{0,1:T(8,128)S(1)}, f32[4,289]{0,1:T(8,128)}, u32[]{:S(2)}, u32[]{:S(2)}) collective-permute-start(f32[4,289]{0,1:T(8,128)S(1)} %pad_maximum_fusion.1), channel_id=1, source_target_pairs={{0,4},{4,8},{8,12},{12,16},{16,20},{20,24},{24,28},{28,32},{32,36}... | collective-permute-start | bytes 13880 | tf_op jit(solution)/shard_map/ppermute | solution.py:45
  46.8 25.3 %copy-start.1 = (bf16[8,288,288]{2,1,0:T(8,128)(2,1)S(1)}, bf16[8,288,288]{2,1,0:T(8,128)(2,1)}, u32[]{:S(2)}) copy-start(bf16[8,288,288]{2,1,0:T(8,128)(2,1)} %shifts_ref.1) | copy-start | bytes 3981316
  46.8 34.3 %all-to-all-start.1 = ((bf16[4,4,80,512]{3,2,1,0:T(8,128)(2,1)}), bf16[4,4,80,512]{3,2,1,0:T(8,128)(2,1)S(1)}, u32[]{:S(2)}, u32[]{:S(2)}) async-start(bf16[4,4,80,512]{3,2,1,0:T(8,128)(2,1)} %broadcast_in_dim.62), calls=%async_computation.1 | async-start | bytes 2621440 | tf_op jit(solution)/shard_map/all_to_all | solution.py:165
  51.0 29.6 %collective-permute-start.4 = (bf16[2,4,72,288]{3,2,1,0:T(8,128)(2,1)}, bf16[2,4,72,288]{3,2,1,0:T(8,128)(2,1)S(1)}, u32[]{:S(2)}, u32[]{:S(2)}) collective-permute-start(bf16[2,4,72,288]{3,2,1,0:T(8,128)(2,1)} %get-tuple-element.32), channel_id=1, source_target_pairs={{0,1},{1,2},{2,3},{3,0},{4,5},{5,6},{6,7},{7,4},{8,9},{9,10},{10,1... | collective-permute-start | bytes 995336 | tf_op jit(solution)/shard_map/ppermute | solution.py:272
  54.5 26.1 %collective-permute-start.5 = (bf16[2,4,72,288]{3,2,1,0:T(8,128)(2,1)}, bf16[2,4,72,288]{3,2,1,0:T(8,128)(2,1)S(1)}, u32[]{:S(2)}, u32[]{:S(2)}) collective-permute-start(bf16[2,4,72,288]{3,2,1,0:T(8,128)(2,1)} %get-tuple-element.33), channel_id=1, source_target_pairs={{0,2},{1,3},{2,0},{3,1},{4,6},{5,7},{6,4},{7,5},{8,10},{9,11},{10,... | collective-permute-start | bytes 995336 | tf_op jit(solution)/shard_map/ppermute | solution.py:272
  59.3 21.3 %collective-permute-start.6 = (bf16[2,4,72,288]{3,2,1,0:T(8,128)(2,1)}, bf16[2,4,72,288]{3,2,1,0:T(8,128)(2,1)S(1)}, u32[]{:S(2)}, u32[]{:S(2)}) collective-permute-start(bf16[2,4,72,288]{3,2,1,0:T(8,128)(2,1)} %get-tuple-element.34), channel_id=1, source_target_pairs={{0,3},{1,0},{2,1},{3,2},{4,7},{5,4},{6,5},{7,6},{8,11},{9,8},{10,9... | collective-permute-start | bytes 995336 | tf_op jit(solution)/shard_map/ppermute | solution.py:272
  62.6 11.3 %collective-permute-start.1 = (bf16[32,128]{1,0:T(8,128)(2,1)S(1)}, bf16[32,128]{1,0:T(8,128)(2,1)S(1)}, u32[]{:S(2)}, u32[]{:S(2)}) collective-permute-start(bf16[32,128]{1,0:T(8,128)(2,1)S(1)} %get-tuple-element.28), channel_id=1, source_target_pairs={{0,128},{128,256},{256,384},{384,0},{1,129},{129,257},{257,385},{3... | collective-permute-start | bytes 24584 | tf_op jit(solution)/shard_map/ppermute | solution.py:272
  64.9 12.1 %collective-permute-start.2 = (bf16[32,128]{1,0:T(8,128)(2,1)S(1)}, bf16[32,128]{1,0:T(8,128)(2,1)S(1)}, u32[]{:S(2)}, u32[]{:S(2)}) collective-permute-start(bf16[32,128]{1,0:T(8,128)(2,1)S(1)} %get-tuple-element.29), channel_id=1, source_target_pairs={{0,256},{128,384},{256,0},{384,128},{1,257},{129,385},{257,1},{385... | collective-permute-start | bytes 24584 | tf_op jit(solution)/shard_map/ppermute | solution.py:272
  70.9 9.7 %copy-start.9 = (bf16[32,128]{1,0:T(8,128)(2,1)S(1)}, bf16[32,128]{1,0:T(8,128)(2,1)}, u32[]{:S(2)}) copy-start(bf16[32,128]{1,0:T(8,128)(2,1)} %get-tuple-element.27) | copy-start | bytes 24580
  73.8 6.7 %collective-permute-start.3 = (bf16[32,128]{1,0:T(8,128)(2,1)S(1)}, bf16[32,128]{1,0:T(8,128)(2,1)S(1)}, u32[]{:S(2)}, u32[]{:S(2)}) collective-permute-start(bf16[32,128]{1,0:T(8,128)(2,1)S(1)} %get-tuple-element.30), channel_id=1, source_target_pairs={{0,384},{128,0},{256,128},{384,256},{1,385},{129,1},{257,129},{385... | collective-permute-start | bytes 24584 | tf_op jit(solution)/shard_map/ppermute | solution.py:272
  81.0 24.8 %collective-permute-start.7 = (bf16[16,80,512]{2,1,0:T(8,128)(2,1)S(1)}, bf16[16,80,512]{2,1,0:T(8,128)(2,1)}, u32[]{:S(2)}, u32[]{:S(2)}) collective-permute-start(bf16[16,80,512]{2,1,0:T(8,128)(2,1)S(1)} %bitcast.80), channel_id=1, source_target_pairs={{0,4},{4,0},{1,5},{5,1},{2,6},{6,2},{3,7},{7,3},{8,12},{12,8},{9,1... | collective-permute-start | bytes 3932168 | tf_op jit(solution)/shard_map/ppermute | solution.py:160
  83.0 16.1 %copy-start.8 = (bf16[72,128]{1,0:T(8,128)(2,1)S(1)}, bf16[72,128]{1,0:T(8,128)(2,1)}, u32[]{:S(2)}) copy-start(bf16[72,128]{1,0:T(8,128)(2,1)} %constant_dynamic-slice_fusion.2) | copy-start | bytes 55300
  83.9 11.7 %all-to-all-start.2 = ((bf16[8,192,128]{2,1,0:T(8,128)(2,1)}), bf16[8,192,128]{2,1,0:T(8,128)(2,1)S(1)}, u32[]{:S(2)}, u32[]{:S(2)}) async-start(bf16[8,192,128]{2,1,0:T(8,128)(2,1)} %bitcast.90), calls=%async_computation.2 | async-start | bytes 786432 | tf_op jit(solution)/shard_map/all_to_all | solution.py:294
  99.9 33.1 %all-to-all-start.3 = ((bf16[16,72,128]{2,1,0:T(8,128)(2,1)}), bf16[16,72,128]{2,1,0:T(8,128)(2,1)S(1)}, u32[]{:S(2)}, u32[]{:S(2)}) async-start(bf16[16,72,128]{2,1,0:T(8,128)(2,1)} %broadcast_in_dim.66), calls=%async_computation.3 | async-start | bytes 589824 | tf_op jit(solution)/shard_map/all_to_all | solution.py:170
  105.8 0.9 copy-start.4
  131.9 1.0 copy-start
  133.0 9.3 %copy-start.2 = (s32[32,1024]{1,0:T(8,128)S(1)}, s32[32,1024]{1,0:T(8,128)}, u32[]{:S(2)}) copy-start(s32[32,1024]{1,0:T(8,128)} %get-tuple-element.46.refs_4_) | copy-start | bytes 393220
  133.0 9.3 %copy-start.3 = (s32[128,256]{1,0:T(8,128)S(1)}, s32[128,256]{1,0:T(8,128)}, u32[]{:S(2)}) copy-start(s32[128,256]{1,0:T(8,128)} %get-tuple-element.47.refs_5_) | copy-start | bytes 393220
  133.0 22.2 %all-to-all-start.4 = ((bf16[16,72,512]{2,1,0:T(8,128)(2,1)}), bf16[16,72,512]{2,1,0:T(8,128)(2,1)}, u32[]{:S(2)}, u32[]{:S(2)}) async-start(bf16[16,72,512]{2,1,0:T(8,128)(2,1)} %bitcast.83), calls=%async_computation.4 | async-start | bytes 2359296 | tf_op jit(solution)/shard_map/all_to_all | solution.py:202
  138.8 3.5 %collective-permute-start.8 = (bf16[16,72,128]{2,1,0:T(8,128)(2,1)S(1)}, bf16[16,72,128]{2,1,0:T(8,128)(2,1)S(1)}, u32[]{:S(2)}, u32[]{:S(2)}) collective-permute-start(bf16[16,72,128]{2,1,0:T(8,128)(2,1)S(1)} %all-to-all-done.3.refs_2_), channel_id=1, source_target_pairs={{0,4},{4,0},{1,5},{5,1},{2,6},{6,2},{3,7},{7,3},{8,12},{12,8},{9,1... | collective-permute-start | bytes 884744 | tf_op jit(solution)/shard_map/ppermute | solution.py:160
  (1 other events, 0.9 us)

commit v3 on v2

--- a/solution.py
+++ b/solution.py
@@ -114,6 +114,8 @@
     lane = lax.broadcasted_iota(jnp.int32, (16, 128), 1) // 8
     lane_bits = [(lane >> b) & 1 == 1 for b in range(4)]
     padded = group_ref.shape[1]
+    by_column = cells > 256
+    place = lax.broadcasted_iota(jnp.int32, (256, cells), 1)
 
     def add_up(q, carry):
         for half in range(2):
@@ -124,18 +126,21 @@
                     group_ref[j, rows, half * 128 : (half + 1) * 128] = array
         for half in range(2):
             lists = dst_ref[pl.ds(pl.multiple_of(q * 16 + half * 8, 8), 8), :]
+            columns = lists.T if by_column else None
             for target in range(2):
                 for couple in range(2):
                     sums = []
                     for j in (target * 4 + couple * 2, target * 4 + couple * 2 + 1):
-                        sums.append(
-                            lax.dot_general(
-                                group_ref[half * 8 + j, 0:height],
-                                one_hot(lists[j : j + 1, :], cells),
-                                (((1,), (1,)), ((), ())),
-                                preferred_element_type=F32,
+                        terms = group_ref[half * 8 + j, 0:height]
+                        if by_column:
+                            hot = (place == columns[:, j : j + 1]).astype(BF16)
+                            one = jnp.dot(terms, hot, preferred_element_type=F32)
+                        else:
+                            hot = one_hot(lists[j : j + 1, :], cells)
+                            one = lax.dot_general(
+                                terms, hot, (((1,), (1,)), ((), ())), preferred_element_type=F32
                             )
-                        )
+                        sums.append(one)
                     distance = (me + 4 - q % 4) % 4
                     start = (distance * 2 + q // 4) * 2 + couple
                     start = pl.multiple_of(start * (2 * height), 2 * height)
@@ -165,9 +170,8 @@
     return lax.all_to_all(copies, axis, 0, 0, tiled=True)
 
 
-def spread_at_once(block):
-    copies = jnp.broadcast_to(block[None], (16,) + block.shape)
-    return lax.all_to_all(copies, ("zh", "zl"), 0, 0, tiled=True)
+def copies_for_z(block):
+    return jnp.broadcast_to(block[None], (16,) + block.shape)
 
 
 def level_partial(pieces, order, src, dst, operators, scale):
@@ -196,11 +200,10 @@
     )(jnp.stack([lax.axis_index("core"), lax.axis_index("comp")]), order, *blocks, src, dst, operators)
 
 
-def summed_over_parts(partial):
+def parts_to_owners(partial):
     groups, width, cells = partial.shape
     pieces = partial.reshape(groups * 4, width // 4, cells)
-    pieces = lax.all_to_all(pieces, ("x", "comp"), 0, 0, tiled=True)
-    return jnp.sum(pieces.astype(F32), axis=0)
+    return lax.all_to_all(pieces, ("x", "comp"), 0, 0, tiled=True)
 
 
 def turned(rows):
@@ -280,8 +283,13 @@
     ]
 
 
-def exchanged(parts, name):
-    return jnp.stack([passed(part, name, distance) for distance, part in enumerate(parts)])
+def exchanged(parts, name, distances):
+    return jnp.stack(
+        [
+            passed(part, name, distance) if distance in distances else part
+            for distance, part in enumerate(parts)
+        ]
+    )
 
 
 def lists_from_chip_and_comp(near, blocks):
@@ -325,30 +333,34 @@
     four = lax.all_to_all(jnp.concatenate([copies, far], axis=1), "zh", 0, 0, tiled=True)
     slot, edge = edge_from_before(fine_moments, child_links)
     near, operators = parts_for(near, "x", 0), operator_parts(translations)
-    four, edge, near, operators = lax.optimization_barrier((four, edge, near, operators))
+    near[1] = passed(near[1], "x", 1)
+    operators[2] = passed(operators[2], "comp", 2)
+    four, near, operators = lax.optimization_barrier((four, near, operators))
     fine = spread_to(four, "zl").reshape((16,) + four.shape[1:])
-    near = exchanged(near, "x")
-    operators = exchanged(operators, "comp").reshape(-1, fine_moments.shape[0])
+    near = exchanged(near, "x", (2, 3))
+    operators = exchanged(operators, "comp", (1, 3)).reshape(-1, fine_moments.shape[0])
     coarse_moments = upward(fine_moments, slot, edge, shifts_up)
-    near, operators, coarse_rows, fine = lax.optimization_barrier(
-        (near, operators, own_rows(coarse_moments), fine)
-    )
+    near, operators, fine = lax.optimization_barrier((near, operators, fine))
     fine_other = other_core(fine)
     fine_src, fine_dst, coarse_src, coarse_dst = slot_lists(*lists_from_chip_and_comp(near, fine))
-    coarse_rows, fine_src = lax.optimization_barrier((coarse_rows, fine_src))
+    coarse = copies_for_z(own_rows(coarse_moments))
+    coarse, fine_src = lax.optimization_barrier((coarse, fine_src))
     place = jnp.arange(16, dtype=jnp.int32)
     order = place % 4 * 4 + place // 4
     fine_partial = level_partial([(fine, fine_other)], order, fine_src, fine_dst, operators, 1.0)
 
-    coarse = spread_at_once(coarse_rows)
+    coarse = lax.all_to_all(coarse, ("zh", "zl"), 0, 0, tiled=True)
     coarse, fine_partial = lax.optimization_barrier((coarse, fine_partial))
     other = other_core(coarse)
     coarse_partial = level_partial(
         [(coarse, other)], place, coarse_src, coarse_dst, operators, 0.5
     )
-    fine_locals = summed_over_parts(fine_partial)
-    coarse_partial, fine_locals = lax.optimization_barrier((coarse_partial, fine_locals))
-    return (fine_locals, coarse_moments, summed_over_parts(coarse_partial))
+    fine_parts = parts_to_owners(fine_partial)
+    coarse_partial, fine_parts = lax.optimization_barrier((coarse_partial, fine_parts))
+    coarse_parts = parts_to_owners(coarse_partial)
+    fine_locals = jnp.sum(fine_parts.astype(F32), axis=0)
+    coarse_locals = jnp.sum(coarse_parts.astype(F32), axis=0)
+    return (fine_locals, coarse_moments, coarse_locals)
 
 
 def solution(mesh):

time: 174 us -> 174 us (level)
  blocking collectives: 12.8 us -> 0 us
  starting transfers between devices: 60.4 us -> 72.1 us
  other arithmetic: 8.38 us -> 11 us
  waiting for transfers between devices: 30.8 us -> 28.9 us
    all_to_all x1 -> x0, blocking collectives: 12.8 us -> none  [summed_over_parts(): pieces = lax.all_to_all(pieces, ('x', 'comp'), 0, 0, tiled=True)]
    ppermute x1, waiting for transfers between devices: 12 us -> 0.01 us  [edge_from_before(): lax.ppermute(edge, CELLS, [(i, i + 1) for i in range(devices - 1)])]
    all_to_all x2 -> x3, starting transfers between devices: 11.8 us -> 19.7 us  [the longest x2 12.8 us: parts_to_owners(): return lax.all_to_all(pieces, ('x', 'comp'), 0, 0, tiled=True)]
    all_to_all x1, waiting for transfers between devices: 0.01 us -> 7.31 us  [spread_to(): return lax.all_to_all(copies, axis, 0, 0, tiled=True)]
    ppermute x6, waiting for transfers between devices: 3.5 us -> 9.43 us  [passed(): lax.ppermute(array, axis, [(i, (i + distance) % count) for i in range(cou...]
    all_to_all x1, waiting for transfers between devices: 8.16 us -> 3.26 us  [lists_from_chip_and_comp(): lax.all_to_all(rows, ('core', 'comp'), 0, 0, tiled=True)]
    all_to_all x2 -> x3, waiting for transfers between devices: 1.3 us -> 5.5 us  [the longest x2 5.5 us: parts_to_owners(): return lax.all_to_all(pieces, ('x', 'comp'), 0, 0, tiled=True)]
    all_to_all x1, starting transfers between devices: 4.14 us -> 7.25 us  [spread_to(): return lax.all_to_all(copies, axis, 0, 0, tiled=True)]
  transfers between devices with their start and end apart: 14 -> 15, of which waited for: 6 -> 10; matrix products, arithmetic and copies ran while one was open for 8% -> 11% of each run, Pallas kernels for 23% -> 23%
where the time goes in v3:
time: 174 us; the launch traced here: 171 us
  starting transfers between devices  72.1 us (41%)
  Pallas kernels  38.7 us (22%)
  waiting for transfers between devices  28.9 us (17%)
  local copies, waits for them, and re-layouts  19 us (11%)
  other arithmetic  11 us (6%)
    pallas_call x2, Pallas kernels, level_partial(): pl.pallas_call(functools.partial(level_kernel, pieces=len(pieces), scale=...  34.9 us
    ppermute x6, starting transfers between devices, passed(): lax.ppermute(array, axis, [(i, (i + distance) % count) for i in range(cou...  19.8 us
    all_to_all x1, starting transfers between devices, per_device(): lax.all_to_all(jnp.concatenate([copies, far], axis=1), 'zh', 0, 0, tiled=...  15.1 us
    all_to_all x2, starting transfers between devices, parts_to_owners(): return lax.all_to_all(pieces, ('x', 'comp'), 0, 0, tiled=True)  12.8 us
    ppermute x6, waiting for transfers between devices, passed(): lax.ppermute(array, axis, [(i, (i + distance) % count) for i in range(cou...  9.43 us
    all_to_all x1, waiting for transfers between devices, spread_to(): return lax.all_to_all(copies, axis, 0, 0, tiled=True)  7.31 us
    all_to_all x1, starting transfers between devices, spread_to(): return lax.all_to_all(copies, axis, 0, 0, tiled=True)  7.25 us
    all_to_all x1, starting transfers between devices, per_device(): coarse = lax.all_to_all(coarse, ('zh', 'zl'), 0, 0, tiled=True)  6.89 us
  transfers between devices with their start and end apart: 15, of which 10 were waited for; matrix products, arithmetic and copies ran while one was open for 11% of the time, Pallas kernels for 23%

profile of v3, /device:TPU:6, one launch (start us, length us, event | category | flops | bytes accessed | tf_op | source)
XLA Modules:
  0.0 170.9 jit_solution(7590353063892265754)
XLA Ops:
  5.5 15.1 %all-to-all-start = ((bf16[4,80,512]{2,1,0:T(8,128)(2,1)}), bf16[4,80,512]{2,1,0:T(8,128)(2,1)S(1)}, u32[]{:S(2)}, u32[]{:S(2)}) async-start(bf16[4,80,512]{2,1,0:T(8,128)(2,1)} %maximum_maximum_fusion.1), calls=%async_computation | async-start | bytes 655360 | tf_op jit(solution)/shard_map/all_to_all | solution.py:333
  22.5 5.1 %collective-permute-start.2 = (bf16[2,4,72,288]{3,2,1,0:T(8,128)(2,1)}, bf16[2,4,72,288]{3,2,1,0:T(8,128)(2,1)S(1)}, u32[]{:S(2)}, u32[]{:S(2)}) collective-permute-start(bf16[2,4,72,288]{3,2,1,0:T(8,128)(2,1)} %get-tuple-element.54), channel_id=1, source_target_pairs={{0,2},{1,3},{2,0},{3,1},{4,6},{5,7},{6,4},{7,5},{8,10},{9,11},{10,... | collective-permute-start | bytes 995336 | tf_op jit(solution)/shard_map/ppermute | solution.py:275
  30.6 2.4 %collective-permute-start.1 = (bf16[32,128]{1,0:T(8,128)(2,1)S(1)}, bf16[32,128]{1,0:T(8,128)(2,1)S(1)}, u32[]{:S(2)}, u32[]{:S(2)}) collective-permute-start(bf16[32,128]{1,0:T(8,128)(2,1)S(1)} %get-tuple-element.60), channel_id=1, source_target_pairs={{0,128},{128,256},{256,384},{384,0},{1,129},{129,257},{257,385},{3... | collective-permute-start | bytes 24584 | tf_op jit(solution)/shard_map/ppermute | solution.py:275
  33.0 3.2 %collective-permute-done.1 = bf16[32,128]{1,0:T(8,128)(2,1)S(1)} collective-permute-done((bf16[32,128]{1,0:T(8,128)(2,1)S(1)}, bf16[32,128]{1,0:T(8,128)(2,1)S(1)}, u32[]{:S(2)}, u32[]{:S(2)}) %collective-permute-start.1) | collective-permute-done | bytes 8224 | tf_op jit(solution)/shard_map/ppermute | solution.py:275
  40.9 7.2 %all-to-all-start.1 = ((bf16[4,4,80,512]{3,2,1,0:T(8,128)(2,1)}), bf16[4,4,80,512]{3,2,1,0:T(8,128)(2,1)S(1)}, u32[]{:S(2)}, u32[]{:S(2)}) async-start(bf16[4,4,80,512]{3,2,1,0:T(8,128)(2,1)} %broadcast_in_dim.63), calls=%async_computation.1 | async-start | bytes 2621440 | tf_op jit(solution)/shard_map/all_to_all | solution.py:170
  49.0 1.9 %collective-permute-start = (f32[4,289]{0,1:T(8,128)}, f32[4,289]{0,1:T(8,128)}, u32[]{:S(2)}, u32[]{:S(2)}) collective-permute-start(f32[4,289]{0,1:T(8,128)} %pad_maximum_fusion.1), channel_id=1, source_target_pairs={{0,4},{4,8},{8,12},{12,16},{16,20},{20,24},{24,28},{28,32},{32,36}... | collective-permute-start | bytes 13880 | tf_op jit(solution)/shard_map/ppermute | solution.py:45
  50.9 3.5 %collective-permute-start.5 = (bf16[2,4,72,288]{3,2,1,0:T(8,128)(2,1)S(1)}, bf16[2,4,72,288]{3,2,1,0:T(8,128)(2,1)S(1)}, u32[]{:S(2)}, u32[]{:S(2)}) collective-permute-start(bf16[2,4,72,288]{3,2,1,0:T(8,128)(2,1)S(1)} %copy-done.8), channel_id=1, source_target_pairs={{0,1},{1,2},{2,3},{3,0},{4,5},{5,6},{6,7},{7,4},{8,9},{9,10},{10,1... | collective-permute-start | bytes 995336 | tf_op jit(solution)/shard_map/ppermute | solution.py:275
  54.4 3.6 %collective-permute-start.6 = (bf16[2,4,72,288]{3,2,1,0:T(8,128)(2,1)S(1)}, bf16[2,4,72,288]{3,2,1,0:T(8,128)(2,1)}, u32[]{:S(2)}, u32[]{:S(2)}) collective-permute-start(bf16[2,4,72,288]{3,2,1,0:T(8,128)(2,1)S(1)} %get-tuple-element.32), channel_id=1, source_target_pairs={{0,3},{1,0},{2,1},{3,2},{4,7},{5,4},{6,5},{7,6},{8,11},{9,8},{10,9... | collective-permute-start | bytes 995336 | tf_op jit(solution)/shard_map/ppermute | solution.py:275
  58.0 3.3 %collective-permute-start.3 = (bf16[32,128]{1,0:T(8,128)(2,1)S(1)}, bf16[32,128]{1,0:T(8,128)(2,1)S(1)}, u32[]{:S(2)}, u32[]{:S(2)}) collective-permute-start(bf16[32,128]{1,0:T(8,128)(2,1)S(1)} %get-tuple-element.27), channel_id=1, source_target_pairs={{0,256},{128,384},{256,0},{384,128},{1,257},{129,385},{257,1},{385... | collective-permute-start | bytes 24584 | tf_op jit(solution)/shard_map/ppermute | solution.py:275
  61.3 1.9 %collective-permute-start.4 = (bf16[32,128]{1,0:T(8,128)(2,1)S(1)}, bf16[32,128]{1,0:T(8,128)(2,1)S(1)}, u32[]{:S(2)}, u32[]{:S(2)}) collective-permute-start(bf16[32,128]{1,0:T(8,128)(2,1)S(1)} %get-tuple-element.28), channel_id=1, source_target_pairs={{0,384},{128,0},{256,128},{384,256},{1,385},{129,1},{257,129},{385... | collective-permute-start | bytes 24584 | tf_op jit(solution)/shard_map/ppermute | solution.py:275
  65.0 3.0 %collective-permute-done.4 = bf16[32,128]{1,0:T(8,128)(2,1)S(1)} collective-permute-done((bf16[32,128]{1,0:T(8,128)(2,1)S(1)}, bf16[32,128]{1,0:T(8,128)(2,1)S(1)}, u32[]{:S(2)}, u32[]{:S(2)}) %collective-permute-start.4) | collective-permute-done | bytes 8224 | tf_op jit(solution)/shard_map/ppermute | solution.py:275
  71.2 7.3 %all-to-all-done.1 = bf16[4,4,80,512]{3,2,1,0:T(8,128)(2,1)S(1)} async-done(((bf16[4,4,80,512]{3,2,1,0:T(8,128)(2,1)}), bf16[4,4,80,512]{3,2,1,0:T(8,128)(2,1)S(1)}, u32[]{:S(2)}, u32[]{:S(2)}) %all-to-all-start.1) | async-done | bytes 1310752 | tf_op jit(solution)/shard_map/all_to_all | solution.py:170
  78.5 1.9 %collective-permute-start.7 = (bf16[16,80,512]{2,1,0:T(8,128)(2,1)S(1)}, bf16[16,80,512]{2,1,0:T(8,128)(2,1)}, u32[]{:S(2)}, u32[]{:S(2)}) collective-permute-start(bf16[16,80,512]{2,1,0:T(8,128)(2,1)S(1)} %bitcast.80), channel_id=1, source_target_pairs={{0,4},{4,0},{1,5},{5,1},{2,6},{6,2},{3,7},{7,3},{8,12},{12,8},{9,1... | collective-permute-start | bytes 3932168 | tf_op jit(solution)/shard_map/ppermute | solution.py:165
  84.4 4.6 %all-to-all-start.2 = ((bf16[8,192,128]{2,1,0:T(8,128)(2,1)}), bf16[8,192,128]{2,1,0:T(8,128)(2,1)S(1)}, u32[]{:S(2)}, u32[]{:S(2)}) async-start(bf16[8,192,128]{2,1,0:T(8,128)(2,1)} %bitcast.89), calls=%async_computation.2 | async-start | bytes 786432 | tf_op jit(solution)/shard_map/all_to_all | solution.py:302
  94.1 3.3 %all-to-all-done.2 = bf16[8,192,128]{2,1,0:T(8,128)(2,1)S(1)} async-done(((bf16[8,192,128]{2,1,0:T(8,128)(2,1)}), bf16[8,192,128]{2,1,0:T(8,128)(2,1)S(1)}, u32[]{:S(2)}, u32[]{:S(2)}) %all-to-all-start.2) | async-done | bytes 393248 | tf_op jit(solution)/shard_map/all_to_all | solution.py:302
  98.8 2.0 %lists.1 = (s32[32,1024]{1,0:T(8,128)}, s32[128,256]{1,0:T(8,128)}, s32[32,1024]{1,0:T(8,128)}, s32[128,256]{1,0:T(8,128)}) custom-call(s32[1]{0:T(128)} %bitcast.8.x_ref, bf16[4,4,2,16,128]{4,3,2,1,0:T(8,128)(2,1)} %bitcast.91, bf16[4,4,32,128]{3,2,1,0:T(8,128)(2,1)} %bitcast.90), custom_call_target="tpu_custom_call" | custom-call | tf_op jit(solution)/shard_map/lists/pallas_call | solution.py:310
  101.6 6.9 %all-to-all-start.3 = ((bf16[16,72,128]{2,1,0:T(8,128)(2,1)}), bf16[16,72,128]{2,1,0:T(8,128)(2,1)S(1)}, u32[]{:S(2)}, u32[]{:S(2)}) async-start(bf16[16,72,128]{2,1,0:T(8,128)(2,1)} %broadcast_in_dim.60), calls=%async_computation.3 | async-start | bytes 589824 | tf_op jit(solution)/shard_map/all_to_all | solution.py:352
  110.3 22.6 %level.2 = bf16[4,288,512]{2,1,0:T(8,128)(2,1)S(1)} custom-call(s32[2]{0:T(128)S(1)} %pad_add_fusion.2.refs_0_, s32[16]{0:T(128)S(1)} %fusion.19.refs_1_, bf16[16,80,512]{2,1,0:T(8,128)(2,1)S(1)} %bitcast.82, bf16[16,80,512]{2,1,0:T(8,128)(2,1)} %collective-permute-done.7.refs_3_, s32[32,1024]{1,0:T(8,128)S(1)} %copy-done.4, s32[128,256]{1,0:T(8,128)S(1)} %copy-done.5, ...), custom_call_target="tpu_custom_call" | custom-call | flops 25600000000 | bytes 6000000 | tf_op jit(solution)/shard_map/level/pallas_call | solution.py:185
  134.0 6.2 %all-to-all-start.4 = ((bf16[16,72,512]{2,1,0:T(8,128)(2,1)}), bf16[16,72,512]{2,1,0:T(8,128)(2,1)}, u32[]{:S(2)}, u32[]{:S(2)}) async-start(bf16[16,72,512]{2,1,0:T(8,128)(2,1)} %bitcast.83), calls=%async_computation.4 | async-start | bytes 2359296 | tf_op jit(solution)/shard_map/all_to_all | solution.py:206
  140.1 1.9 %collective-permute-start.8 = (bf16[16,72,128]{2,1,0:T(8,128)(2,1)S(1)}, bf16[16,72,128]{2,1,0:T(8,128)(2,1)S(1)}, u32[]{:S(2)}, u32[]{:S(2)}) collective-permute-start(bf16[16,72,128]{2,1,0:T(8,128)(2,1)S(1)} %all-to-all-done.3.refs_2_), channel_id=1, source_target_pairs={{0,4},{4,0},{1,5},{5,1},{2,6},{6,2},{3,7},{7,3},{8,12},{12,8},{9,1... | collective-permute-start | bytes 884744 | tf_op jit(solution)/shard_map/ppermute | solution.py:165
  143.6 12.3 %level.3 = bf16[4,288,128]{2,1,0:T(8,128)(2,1)} custom-call(s32[2]{0:T(128)S(1)} %pad_add_fusion.2.refs_0_, s32[16]{0:T(128)S(1)} %iota.5.refs_1_, bf16[16,72,128]{2,1,0:T(8,128)(2,1)S(1)} %all-to-all-done.3.refs_2_, bf16[16,72,128]{2,1,0:T(8,128)(2,1)S(1)} %collective-permute-done.8.refs_3_, s32[32,1024]{1,0:T(8,128)S(1)} %copy-done.2, ...), custom_call_target="tpu_custom_call" | custom-call | flops 6400000000 | bytes 6000000 | tf_op jit(solution)/shard_map/level/pallas_call | solution.py:185
  156.5 6.7 %all-to-all-start.5 = ((bf16[16,72,128]{2,1,0:T(8,128)(2,1)}), bf16[16,72,128]{2,1,0:T(8,128)(2,1)S(1)}, u32[]{:S(2)}, u32[]{:S(2)}) async-start(bf16[16,72,128]{2,1,0:T(8,128)(2,1)} %bitcast.49), calls=%async_computation.5 | async-start | bytes 589824 | tf_op jit(solution)/shard_map/all_to_all | solution.py:206
  163.2 2.1 %convert_reduce_fusion = f32[72,512]{1,0:T(8,128)} fusion(bf16[16,72,512]{2,1,0:T(8,128)(2,1)} %all-to-all-done.4), kind=kLoop, calls=%fused_computation.8 | loop fusion | flops 1142784 | bytes 1327104 | tf_op jit(solution)/shard_map/reduce_sum | solution.py:361
  165.3 4.9 %all-to-all-done.5 = bf16[16,72,128]{2,1,0:T(8,128)(2,1)S(1)} async-done(((bf16[16,72,128]{2,1,0:T(8,128)(2,1)}), bf16[16,72,128]{2,1,0:T(8,128)(2,1)S(1)}, u32[]{:S(2)}, u32[]{:S(2)}) %all-to-all-start.5) | async-done | bytes 294944 | tf_op jit(solution)/shard_map/all_to_all | solution.py:206
  (93 shorter events, 36.9 us)
Async XLA Ops:
  0.6 4.0 %copy-start.7 = (bf16[288,512]{1,0:T(8,128)(2,1)S(1)}, bf16[288,512]{1,0:T(8,128)(2,1)}, u32[]{:S(2)}) copy-start(bf16[288,512]{1,0:T(8,128)(2,1)} %param.6) | copy-start | bytes 884740
  3.1 17.4 %copy-start.6 = (bf16[4,288,288]{2,1,0:T(8,128)(2,1)S(1)}, bf16[4,288,288]{2,1,0:T(8,128)(2,1)}, u32[]{:S(2)}) copy-start(bf16[4,288,288]{2,1,0:T(8,128)(2,1)} %param.7) | copy-start | bytes 1990660
  5.5 34.2 %all-to-all-start = ((bf16[4,80,512]{2,1,0:T(8,128)(2,1)}), bf16[4,80,512]{2,1,0:T(8,128)(2,1)S(1)}, u32[]{:S(2)}, u32[]{:S(2)}) async-start(bf16[4,80,512]{2,1,0:T(8,128)(2,1)} %maximum_maximum_fusion.1), calls=%async_computation | async-start | bytes 655360 | tf_op jit(solution)/shard_map/all_to_all | solution.py:333
  22.5 15.2 %collective-permute-start.2 = (bf16[2,4,72,288]{3,2,1,0:T(8,128)(2,1)}, bf16[2,4,72,288]{3,2,1,0:T(8,128)(2,1)S(1)}, u32[]{:S(2)}, u32[]{:S(2)}) collective-permute-start(bf16[2,4,72,288]{3,2,1,0:T(8,128)(2,1)} %get-tuple-element.54), channel_id=1, source_target_pairs={{0,2},{1,3},{2,0},{3,1},{4,6},{5,7},{6,4},{7,5},{8,10},{9,11},{10,... | collective-permute-start | bytes 995336 | tf_op jit(solution)/shard_map/ppermute | solution.py:275
  30.6 5.5 %collective-permute-start.1 = (bf16[32,128]{1,0:T(8,128)(2,1)S(1)}, bf16[32,128]{1,0:T(8,128)(2,1)S(1)}, u32[]{:S(2)}, u32[]{:S(2)}) collective-permute-start(bf16[32,128]{1,0:T(8,128)(2,1)S(1)} %get-tuple-element.60), channel_id=1, source_target_pairs={{0,128},{128,256},{256,384},{384,0},{1,129},{129,257},{257,385},{3... | collective-permute-start | bytes 24584 | tf_op jit(solution)/shard_map/ppermute | solution.py:275
  37.8 1.9 %copy-start.9 = (bf16[2,4,72,288]{3,2,1,0:T(8,128)(2,1)}, bf16[2,4,72,288]{3,2,1,0:T(8,128)(2,1)S(1)}, u32[]{:S(2)}) copy-start(bf16[2,4,72,288]{3,2,1,0:T(8,128)(2,1)S(1)} %collective-permute-done.2) | copy-start | bytes 995332
  39.7 8.5 %copy-start.11 = (s32[2,512]{1,0:T(2,128)S(1)}, s32[2,512]{1,0:T(2,128)}, u32[]{:S(2)}) copy-start(s32[2,512]{1,0:T(2,128)} %param.11) | copy-start | bytes 12292
  40.9 10.0 %copy-start.8 = (bf16[2,4,72,288]{3,2,1,0:T(8,128)(2,1)S(1)}, bf16[2,4,72,288]{3,2,1,0:T(8,128)(2,1)}, u32[]{:S(2)}) copy-start(bf16[2,4,72,288]{3,2,1,0:T(8,128)(2,1)} %get-tuple-element.30) | copy-start | bytes 995332
  40.9 37.6 %all-to-all-start.1 = ((bf16[4,4,80,512]{3,2,1,0:T(8,128)(2,1)}), bf16[4,4,80,512]{3,2,1,0:T(8,128)(2,1)S(1)}, u32[]{:S(2)}, u32[]{:S(2)}) async-start(bf16[4,4,80,512]{3,2,1,0:T(8,128)(2,1)} %broadcast_in_dim.63), calls=%async_computation.1 | async-start | bytes 2621440 | tf_op jit(solution)/shard_map/all_to_all | solution.py:170
  49.0 31.4 %collective-permute-start = (f32[4,289]{0,1:T(8,128)}, f32[4,289]{0,1:T(8,128)}, u32[]{:S(2)}, u32[]{:S(2)}) collective-permute-start(f32[4,289]{0,1:T(8,128)} %pad_maximum_fusion.1), channel_id=1, source_target_pairs={{0,4},{4,8},{8,12},{12,16},{16,20},{20,24},{24,28},{28,32},{32,36}... | collective-permute-start | bytes 13880 | tf_op jit(solution)/shard_map/ppermute | solution.py:45
  50.9 17.8 %collective-permute-start.5 = (bf16[2,4,72,288]{3,2,1,0:T(8,128)(2,1)S(1)}, bf16[2,4,72,288]{3,2,1,0:T(8,128)(2,1)S(1)}, u32[]{:S(2)}, u32[]{:S(2)}) collective-permute-start(bf16[2,4,72,288]{3,2,1,0:T(8,128)(2,1)S(1)} %copy-done.8), channel_id=1, source_target_pairs={{0,1},{1,2},{2,3},{3,0},{4,5},{5,6},{6,7},{7,4},{8,9},{9,10},{10,1... | collective-permute-start | bytes 995336 | tf_op jit(solution)/shard_map/ppermute | solution.py:275
  54.4 14.3 %collective-permute-start.6 = (bf16[2,4,72,288]{3,2,1,0:T(8,128)(2,1)S(1)}, bf16[2,4,72,288]{3,2,1,0:T(8,128)(2,1)}, u32[]{:S(2)}, u32[]{:S(2)}) collective-permute-start(bf16[2,4,72,288]{3,2,1,0:T(8,128)(2,1)S(1)} %get-tuple-element.32), channel_id=1, source_target_pairs={{0,3},{1,0},{2,1},{3,2},{4,7},{5,4},{6,5},{7,6},{8,11},{9,8},{10,9... | collective-permute-start | bytes 995336 | tf_op jit(solution)/shard_map/ppermute | solution.py:275
  58.0 7.0 %collective-permute-start.3 = (bf16[32,128]{1,0:T(8,128)(2,1)S(1)}, bf16[32,128]{1,0:T(8,128)(2,1)S(1)}, u32[]{:S(2)}, u32[]{:S(2)}) collective-permute-start(bf16[32,128]{1,0:T(8,128)(2,1)S(1)} %get-tuple-element.27), channel_id=1, source_target_pairs={{0,256},{128,384},{256,0},{384,128},{1,257},{129,385},{257,1},{385... | collective-permute-start | bytes 24584 | tf_op jit(solution)/shard_map/ppermute | solution.py:275
  61.3 6.8 %collective-permute-start.4 = (bf16[32,128]{1,0:T(8,128)(2,1)S(1)}, bf16[32,128]{1,0:T(8,128)(2,1)S(1)}, u32[]{:S(2)}, u32[]{:S(2)}) collective-permute-start(bf16[32,128]{1,0:T(8,128)(2,1)S(1)} %get-tuple-element.28), channel_id=1, source_target_pairs={{0,384},{128,0},{256,128},{384,256},{1,385},{129,1},{257,129},{385... | collective-permute-start | bytes 24584 | tf_op jit(solution)/shard_map/ppermute | solution.py:275
  78.5 30.0 %collective-permute-start.7 = (bf16[16,80,512]{2,1,0:T(8,128)(2,1)S(1)}, bf16[16,80,512]{2,1,0:T(8,128)(2,1)}, u32[]{:S(2)}, u32[]{:S(2)}) collective-permute-start(bf16[16,80,512]{2,1,0:T(8,128)(2,1)S(1)} %bitcast.80), channel_id=1, source_target_pairs={{0,4},{4,0},{1,5},{5,1},{2,6},{6,2},{3,7},{7,3},{8,12},{12,8},{9,1... | collective-permute-start | bytes 3932168 | tf_op jit(solution)/shard_map/ppermute | solution.py:165
  84.4 12.9 %all-to-all-start.2 = ((bf16[8,192,128]{2,1,0:T(8,128)(2,1)}), bf16[8,192,128]{2,1,0:T(8,128)(2,1)S(1)}, u32[]{:S(2)}, u32[]{:S(2)}) async-start(bf16[8,192,128]{2,1,0:T(8,128)(2,1)} %bitcast.89), calls=%async_computation.2 | async-start | bytes 786432 | tf_op jit(solution)/shard_map/all_to_all | solution.py:302
  90.1 1.5 copy-start.1
  101.6 32.4 %all-to-all-start.3 = ((bf16[16,72,128]{2,1,0:T(8,128)(2,1)}), bf16[16,72,128]{2,1,0:T(8,128)(2,1)S(1)}, u32[]{:S(2)}, u32[]{:S(2)}) async-start(bf16[16,72,128]{2,1,0:T(8,128)(2,1)} %broadcast_in_dim.60), calls=%async_computation.3 | async-start | bytes 589824 | tf_op jit(solution)/shard_map/all_to_all | solution.py:352
  132.9 1.0 copy-start
  134.0 9.6 %copy-start.2 = (s32[32,1024]{1,0:T(8,128)S(1)}, s32[32,1024]{1,0:T(8,128)}, u32[]{:S(2)}) copy-start(s32[32,1024]{1,0:T(8,128)} %get-tuple-element.42.refs_4_) | copy-start | bytes 393220
  134.0 9.6 %copy-start.3 = (s32[128,256]{1,0:T(8,128)S(1)}, s32[128,256]{1,0:T(8,128)}, u32[]{:S(2)}) copy-start(s32[128,256]{1,0:T(8,128)} %get-tuple-element.43.refs_5_) | copy-start | bytes 393220
  134.0 22.5 %all-to-all-start.4 = ((bf16[16,72,512]{2,1,0:T(8,128)(2,1)}), bf16[16,72,512]{2,1,0:T(8,128)(2,1)}, u32[]{:S(2)}, u32[]{:S(2)}) async-start(bf16[16,72,512]{2,1,0:T(8,128)(2,1)} %bitcast.83), calls=%async_computation.4 | async-start | bytes 2359296 | tf_op jit(solution)/shard_map/all_to_all | solution.py:206
  140.1 3.5 %collective-permute-start.8 = (bf16[16,72,128]{2,1,0:T(8,128)(2,1)S(1)}, bf16[16,72,128]{2,1,0:T(8,128)(2,1)S(1)}, u32[]{:S(2)}, u32[]{:S(2)}) collective-permute-start(bf16[16,72,128]{2,1,0:T(8,128)(2,1)S(1)} %all-to-all-done.3.refs_2_), channel_id=1, source_target_pairs={{0,4},{4,0},{1,5},{5,1},{2,6},{6,2},{3,7},{7,3},{8,12},{12,8},{9,1... | collective-permute-start | bytes 884744 | tf_op jit(solution)/shard_map/ppermute | solution.py:165
  156.5 13.7 %all-to-all-start.5 = ((bf16[16,72,128]{2,1,0:T(8,128)(2,1)}), bf16[16,72,128]{2,1,0:T(8,128)(2,1)S(1)}, u32[]{:S(2)}, u32[]{:S(2)}) async-start(bf16[16,72,128]{2,1,0:T(8,128)(2,1)} %bitcast.49), calls=%async_computation.5 | async-start | bytes 589824 | tf_op jit(solution)/shard_map/all_to_all | solution.py:206
  (3 other events, 2.6 us)

commit v4 on v3

--- a/solution.py
+++ b/solution.py
@@ -217,7 +217,7 @@
     return rows
 
 
-def lists_kernel(x_ref, near_ref, far_ref, *out_refs):
+def lists_kernel(place_ref, near_ref, far_ref, *out_refs):
     lane = lax.broadcasted_iota(jnp.int32, (16, 128), 1) // 8
     lane_bits = [(lane >> b) & 1 == 1 for b in range(4)]
 
@@ -226,7 +226,11 @@
 
     for part in range(4):
         for half in range(2):
-            near_lists = [cells_of(near_ref[part, (x_ref[0] + 4 - g) % 4, half]) for g in range(4)]
+            near_lists = []
+            for g in range(4):
+                first = 64 + ((place_ref[0] + 4 - g) % 4 * 2 + half) * 16
+                rows = pl.ds(pl.multiple_of(first, 16), 16)
+                near_lists.append(cells_of(near_ref[place_ref[1], part, rows, :]))
             for level in range(2):
                 src_ref, dst_ref = out_refs[2 * level : 2 * level + 2]
                 lanes = slice(half * 128, (half + 1) * 128)
@@ -292,17 +296,19 @@
     )
 
 
-def lists_from_chip_and_comp(near, blocks):
+def lists_message(near, blocks):
     rows = blocks[:, 72:].reshape(4, 4, 2, 4, -1)
     rows = lax.dynamic_slice_in_dim(rows, lax.axis_index("zl") * 128, 128, 4)
     rows = rows.transpose(2, 0, 1, 3, 4).reshape(2, 64, 128)
     near = jnp.broadcast_to(near.reshape(1, 128, 128), (2, 128, 128))
     rows = jnp.concatenate([rows, near], axis=1)
-    rows = jnp.broadcast_to(rows[:, None], (2, 4, 192, 128)).reshape(8, 192, 128)
-    rows = lax.all_to_all(rows, ("core", "comp"), 0, 0, tiled=True).reshape(2, 4, 192, 128)
-    near = lax.dynamic_index_in_dim(rows[:, :, 64:], lax.axis_index("core"), 0, keepdims=False)
+    return jnp.broadcast_to(rows[:, None], (2, 4, 192, 128)).reshape(8, 192, 128)
+
+
+def lists_from_chip_and_comp(message):
+    rows = lax.all_to_all(message, ("core", "comp"), 0, 0, tiled=True).reshape(2, 4, 192, 128)
     far = rows[:, :, :64].reshape(2, 4, 4, 4, 4, 128).transpose(1, 4, 3, 2, 0, 5)
-    return near.reshape(4, 4, 2, 16, 128), far.reshape(4, 4, 32, 128)
+    return rows, far.reshape(4, 4, 32, 128)
 
 
 def slot_lists(near, far):
@@ -317,7 +323,7 @@
         ]
         * 2,
         name="lists",
-    )(lax.axis_index("x").reshape(1), near, far)
+    )(jnp.stack([lax.axis_index("x"), lax.axis_index("core")]), near, far)
 
 
 def operator_parts(translations):
@@ -341,8 +347,10 @@
     operators = exchanged(operators, "comp", (1, 3)).reshape(-1, fine_moments.shape[0])
     coarse_moments = upward(fine_moments, slot, edge, shifts_up)
     near, operators, fine = lax.optimization_barrier((near, operators, fine))
+    message, fine = lax.optimization_barrier((lists_message(near, fine), fine))
     fine_other = other_core(fine)
-    fine_src, fine_dst, coarse_src, coarse_dst = slot_lists(*lists_from_chip_and_comp(near, fine))
+    lists = slot_lists(*lists_from_chip_and_comp(message))
+    fine_src, fine_dst, coarse_src, coarse_dst = lists
     coarse = copies_for_z(own_rows(coarse_moments))
     coarse, fine_src = lax.optimization_barrier((coarse, fine_src))
     place = jnp.arange(16, dtype=jnp.int32)

time: 174 us -> 175 us (level)
    all_to_all x1, waiting for transfers between devices: 7.31 us -> 9.96 us  [spread_to(): return lax.all_to_all(copies, axis, 0, 0, tiled=True)]
    ppermute x6, waiting for transfers between devices: 9.43 us -> 6.99 us  [passed(): lax.ppermute(array, axis, [(i, (i + distance) % count) for i in range(cou...]
  transfers between devices with their start and end apart: 15 -> 15, of which waited for: 10 -> 9; matrix products, arithmetic and copies ran while one was open for 11% -> 11% of each run, Pallas kernels for 23% -> 23%
where the time goes in v4:
time: 175 us; the launch traced here: 172 us
  starting transfers between devices  72.1 us (41%)
  Pallas kernels  38.8 us (22%)
  waiting for transfers between devices  29.3 us (17%)
  local copies, waits for them, and re-layouts  18.5 us (11%)
  other arithmetic  12.2 us (7%)
    pallas_call x2, Pallas kernels, level_partial(): pl.pallas_call(functools.partial(level_kernel, pieces=len(pieces), scale=...  34.9 us
    ppermute x6, starting transfers between devices, passed(): lax.ppermute(array, axis, [(i, (i + distance) % count) for i in range(cou...  19.8 us
    all_to_all x1, starting transfers between devices, per_device(): lax.all_to_all(jnp.concatenate([copies, far], axis=1), 'zh', 0, 0, tiled=...  15.1 us
    all_to_all x2, starting transfers between devices, parts_to_owners(): return lax.all_to_all(pieces, ('x', 'comp'), 0, 0, tiled=True)  12.8 us
    all_to_all x1, waiting for transfers between devices, spread_to(): return lax.all_to_all(copies, axis, 0, 0, tiled=True)  9.96 us
    all_to_all x1, starting transfers between devices, spread_to(): return lax.all_to_all(copies, axis, 0, 0, tiled=True)  7.25 us
    ppermute x6, waiting for transfers between devices, passed(): lax.ppermute(array, axis, [(i, (i + distance) % count) for i in range(cou...  6.99 us
    all_to_all x1, starting transfers between devices, per_device(): coarse = lax.all_to_all(coarse, ('zh', 'zl'), 0, 0, tiled=True)  6.9 us
  transfers between devices with their start and end apart: 15, of which 9 were waited for; matrix products, arithmetic and copies ran while one was open for 11% of the time, Pallas kernels for 23%

profile of v4, /device:TPU:6, one launch (start us, length us, event | category | flops | bytes accessed | tf_op | source)
XLA Modules:
  0.0 171.9 jit_solution(2678564283207186712)
XLA Ops:
  5.5 15.1 %all-to-all-start = ((bf16[4,80,512]{2,1,0:T(8,128)(2,1)}), bf16[4,80,512]{2,1,0:T(8,128)(2,1)S(1)}, u32[]{:S(2)}, u32[]{:S(2)}) async-start(bf16[4,80,512]{2,1,0:T(8,128)(2,1)} %maximum_maximum_fusion.1), calls=%async_computation | async-start | bytes 655360 | tf_op jit(solution)/shard_map/all_to_all | solution.py:339
  22.5 5.1 %collective-permute-start.2 = (bf16[2,4,72,288]{3,2,1,0:T(8,128)(2,1)}, bf16[2,4,72,288]{3,2,1,0:T(8,128)(2,1)S(1)}, u32[]{:S(2)}, u32[]{:S(2)}) collective-permute-start(bf16[2,4,72,288]{3,2,1,0:T(8,128)(2,1)} %get-tuple-element.58), channel_id=1, source_target_pairs={{0,2},{1,3},{2,0},{3,1},{4,6},{5,7},{6,4},{7,5},{8,10},{9,11},{10,... | collective-permute-start | bytes 995336 | tf_op jit(solution)/shard_map/ppermute | solution.py:279
  30.6 2.4 %collective-permute-start.1 = (bf16[32,128]{1,0:T(8,128)(2,1)S(1)}, bf16[32,128]{1,0:T(8,128)(2,1)S(1)}, u32[]{:S(2)}, u32[]{:S(2)}) collective-permute-start(bf16[32,128]{1,0:T(8,128)(2,1)S(1)} %get-tuple-element.64), channel_id=1, source_target_pairs={{0,128},{128,256},{256,384},{384,0},{1,129},{129,257},{257,385},{3... | collective-permute-start | bytes 24584 | tf_op jit(solution)/shard_map/ppermute | solution.py:279
  33.0 3.2 %collective-permute-done.1 = bf16[32,128]{1,0:T(8,128)(2,1)S(1)} collective-permute-done((bf16[32,128]{1,0:T(8,128)(2,1)S(1)}, bf16[32,128]{1,0:T(8,128)(2,1)S(1)}, u32[]{:S(2)}, u32[]{:S(2)}) %collective-permute-start.1) | collective-permute-done | bytes 8224 | tf_op jit(solution)/shard_map/ppermute | solution.py:279
  40.9 7.2 %all-to-all-start.1 = ((bf16[4,4,80,512]{3,2,1,0:T(8,128)(2,1)}), bf16[4,4,80,512]{3,2,1,0:T(8,128)(2,1)S(1)}, u32[]{:S(2)}, u32[]{:S(2)}) async-start(bf16[4,4,80,512]{3,2,1,0:T(8,128)(2,1)} %broadcast_in_dim.63), calls=%async_computation.1 | async-start | bytes 2621440 | tf_op jit(solution)/shard_map/all_to_all | solution.py:170
  48.8 3.5 %collective-permute-start.5 = (bf16[2,4,72,288]{3,2,1,0:T(8,128)(2,1)S(1)}, bf16[2,4,72,288]{3,2,1,0:T(8,128)(2,1)S(1)}, u32[]{:S(2)}, u32[]{:S(2)}) collective-permute-start(bf16[2,4,72,288]{3,2,1,0:T(8,128)(2,1)S(1)} %copy-done.8), channel_id=1, source_target_pairs={{0,1},{1,2},{2,3},{3,0},{4,5},{5,6},{6,7},{7,4},{8,9},{9,10},{10,1... | collective-permute-start | bytes 995336 | tf_op jit(solution)/shard_map/ppermute | solution.py:279
  52.3 3.6 %collective-permute-start.6 = (bf16[2,4,72,288]{3,2,1,0:T(8,128)(2,1)S(1)}, bf16[2,4,72,288]{3,2,1,0:T(8,128)(2,1)}, u32[]{:S(2)}, u32[]{:S(2)}) collective-permute-start(bf16[2,4,72,288]{3,2,1,0:T(8,128)(2,1)S(1)} %get-tuple-element.34), channel_id=1, source_target_pairs={{0,3},{1,0},{2,1},{3,2},{4,7},{5,4},{6,5},{7,6},{8,11},{9,8},{10,9... | collective-permute-start | bytes 995336 | tf_op jit(solution)/shard_map/ppermute | solution.py:279
  56.0 3.3 %collective-permute-start.3 = (bf16[32,128]{1,0:T(8,128)(2,1)S(1)}, bf16[32,128]{1,0:T(8,128)(2,1)S(1)}, u32[]{:S(2)}, u32[]{:S(2)}) collective-permute-start(bf16[32,128]{1,0:T(8,128)(2,1)S(1)} %get-tuple-element.29), channel_id=1, source_target_pairs={{0,256},{128,384},{256,0},{384,128},{1,257},{129,385},{257,1},{385... | collective-permute-start | bytes 24584 | tf_op jit(solution)/shard_map/ppermute | solution.py:279
  59.3 1.9 %collective-permute-start.4 = (bf16[32,128]{1,0:T(8,128)(2,1)S(1)}, bf16[32,128]{1,0:T(8,128)(2,1)S(1)}, u32[]{:S(2)}, u32[]{:S(2)}) collective-permute-start(bf16[32,128]{1,0:T(8,128)(2,1)S(1)} %get-tuple-element.30), channel_id=1, source_target_pairs={{0,384},{128,0},{256,128},{384,256},{1,385},{129,1},{257,129},{385... | collective-permute-start | bytes 24584 | tf_op jit(solution)/shard_map/ppermute | solution.py:279
  61.9 1.9 %collective-permute-start = (f32[4,289]{0,1:T(8,128)}, f32[4,289]{0,1:T(8,128)}, u32[]{:S(2)}, u32[]{:S(2)}) collective-permute-start(f32[4,289]{0,1:T(8,128)} %pad_maximum_fusion.1), channel_id=1, source_target_pairs={{0,4},{4,8},{8,12},{12,16},{16,20},{20,24},{24,28},{28,32},{32,36}... | collective-permute-start | bytes 13880 | tf_op jit(solution)/shard_map/ppermute | solution.py:45
  63.8 2.2 %collective-permute-done.4 = bf16[32,128]{1,0:T(8,128)(2,1)S(1)} collective-permute-done((bf16[32,128]{1,0:T(8,128)(2,1)S(1)}, bf16[32,128]{1,0:T(8,128)(2,1)S(1)}, u32[]{:S(2)}, u32[]{:S(2)}) %collective-permute-start.4) | collective-permute-done | bytes 8224 | tf_op jit(solution)/shard_map/ppermute | solution.py:279
  68.5 10.0 %all-to-all-done.1 = bf16[4,4,80,512]{3,2,1,0:T(8,128)(2,1)S(1)} async-done(((bf16[4,4,80,512]{3,2,1,0:T(8,128)(2,1)}), bf16[4,4,80,512]{3,2,1,0:T(8,128)(2,1)S(1)}, u32[]{:S(2)}, u32[]{:S(2)}) %all-to-all-start.1) | async-done | bytes 1310752 | tf_op jit(solution)/shard_map/all_to_all | solution.py:170
  79.4 1.9 %collective-permute-start.7 = (bf16[16,80,512]{2,1,0:T(8,128)(2,1)S(1)}, bf16[16,80,512]{2,1,0:T(8,128)(2,1)}, u32[]{:S(2)}, u32[]{:S(2)}) collective-permute-start(bf16[16,80,512]{2,1,0:T(8,128)(2,1)S(1)} %bitcast.80), channel_id=1, source_target_pairs={{0,4},{4,0},{1,5},{5,1},{2,6},{6,2},{3,7},{7,3},{8,12},{12,8},{9,1... | collective-permute-start | bytes 3932168 | tf_op jit(solution)/shard_map/ppermute | solution.py:165
  85.1 4.6 %all-to-all-start.2 = ((bf16[8,192,128]{2,1,0:T(8,128)(2,1)}), bf16[8,192,128]{2,1,0:T(8,128)(2,1)}, u32[]{:S(2)}, u32[]{:S(2)}) async-start(bf16[8,192,128]{2,1,0:T(8,128)(2,1)} %bitcast.42), calls=%async_computation.2 | async-start | bytes 786432 | tf_op jit(solution)/shard_map/all_to_all | solution.py:309
  94.7 3.4 %all-to-all-done.2 = bf16[8,192,128]{2,1,0:T(8,128)(2,1)} async-done(((bf16[8,192,128]{2,1,0:T(8,128)(2,1)}), bf16[8,192,128]{2,1,0:T(8,128)(2,1)}, u32[]{:S(2)}, u32[]{:S(2)}) %all-to-all-start.2) | async-done | bytes 393248 | tf_op jit(solution)/shard_map/all_to_all | solution.py:309
  99.8 2.1 %lists.1 = (s32[32,1024]{1,0:T(8,128)}, s32[128,256]{1,0:T(8,128)}, s32[32,1024]{1,0:T(8,128)}, s32[128,256]{1,0:T(8,128)}) custom-call(s32[2]{0:T(128)} %pad_add_fusion.3.place_ref, bf16[2,4,192,128]{3,2,1,0:T(8,128)(2,1)} %bitcast.43.near_ref, bf16[4,4,32,128]{3,2,1,0:T(8,128)(2,1)} %bitcast.86), custom_call_target="tpu_custom_call" | custom-call | tf_op jit(solution)/shard_map/lists/pallas_call | solution.py:316
  102.7 6.9 %all-to-all-start.3 = ((bf16[16,72,128]{2,1,0:T(8,128)(2,1)}), bf16[16,72,128]{2,1,0:T(8,128)(2,1)S(1)}, u32[]{:S(2)}, u32[]{:S(2)}) async-start(bf16[16,72,128]{2,1,0:T(8,128)(2,1)} %broadcast_in_dim.60), calls=%async_computation.3 | async-start | bytes 589824 | tf_op jit(solution)/shard_map/all_to_all | solution.py:360
  111.4 22.6 %level.2 = bf16[4,288,512]{2,1,0:T(8,128)(2,1)S(1)} custom-call(s32[2]{0:T(128)S(1)} %pad_add_fusion.2.refs_0_, s32[16]{0:T(128)S(1)} %fusion.19.refs_1_, bf16[16,80,512]{2,1,0:T(8,128)(2,1)S(1)} %bitcast.81, bf16[16,80,512]{2,1,0:T(8,128)(2,1)} %collective-permute-done.7.refs_3_, s32[32,1024]{1,0:T(8,128)S(1)} %copy-done.4, s32[128,256]{1,0:T(8,128)S(1)} %copy-done.5, ...), custom_call_target="tpu_custom_call" | custom-call | flops 25600000000 | bytes 6000000 | tf_op jit(solution)/shard_map/level/pallas_call | solution.py:185
  135.0 6.2 %all-to-all-start.4 = ((bf16[16,72,512]{2,1,0:T(8,128)(2,1)}), bf16[16,72,512]{2,1,0:T(8,128)(2,1)}, u32[]{:S(2)}, u32[]{:S(2)}) async-start(bf16[16,72,512]{2,1,0:T(8,128)(2,1)} %bitcast.82), calls=%async_computation.4 | async-start | bytes 2359296 | tf_op jit(solution)/shard_map/all_to_all | solution.py:206
  141.2 1.9 %collective-permute-start.8 = (bf16[16,72,128]{2,1,0:T(8,128)(2,1)S(1)}, bf16[16,72,128]{2,1,0:T(8,128)(2,1)S(1)}, u32[]{:S(2)}, u32[]{:S(2)}) collective-permute-start(bf16[16,72,128]{2,1,0:T(8,128)(2,1)S(1)} %all-to-all-done.3.refs_2_), channel_id=1, source_target_pairs={{0,4},{4,0},{1,5},{5,1},{2,6},{6,2},{3,7},{7,3},{8,12},{12,8},{9,1... | collective-permute-start | bytes 884744 | tf_op jit(solution)/shard_map/ppermute | solution.py:165
  144.7 12.3 %level.3 = bf16[4,288,128]{2,1,0:T(8,128)(2,1)} custom-call(s32[2]{0:T(128)S(1)} %pad_add_fusion.2.refs_0_, s32[16]{0:T(128)S(1)} %iota.5.refs_1_, bf16[16,72,128]{2,1,0:T(8,128)(2,1)S(1)} %all-to-all-done.3.refs_2_, bf16[16,72,128]{2,1,0:T(8,128)(2,1)S(1)} %collective-permute-done.8.refs_3_, s32[32,1024]{1,0:T(8,128)S(1)} %copy-done.2, ...), custom_call_target="tpu_custom_call" | custom-call | flops 6400000000 | bytes 6000000 | tf_op jit(solution)/shard_map/level/pallas_call | solution.py:185
  157.5 6.7 %all-to-all-start.5 = ((bf16[16,72,128]{2,1,0:T(8,128)(2,1)}), bf16[16,72,128]{2,1,0:T(8,128)(2,1)S(1)}, u32[]{:S(2)}, u32[]{:S(2)}) async-start(bf16[16,72,128]{2,1,0:T(8,128)(2,1)} %bitcast.48), calls=%async_computation.5 | async-start | bytes 589824 | tf_op jit(solution)/shard_map/all_to_all | solution.py:206
  164.2 2.1 %convert_reduce_fusion = f32[72,512]{1,0:T(8,128)} fusion(bf16[16,72,512]{2,1,0:T(8,128)(2,1)} %all-to-all-done.4), kind=kLoop, calls=%fused_computation.8 | loop fusion | flops 1142784 | bytes 1327104 | tf_op jit(solution)/shard_map/reduce_sum | solution.py:369
  166.3 4.9 %all-to-all-done.5 = bf16[16,72,128]{2,1,0:T(8,128)(2,1)S(1)} async-done(((bf16[16,72,128]{2,1,0:T(8,128)(2,1)}), bf16[16,72,128]{2,1,0:T(8,128)(2,1)S(1)}, u32[]{:S(2)}, u32[]{:S(2)}) %all-to-all-start.5) | async-done | bytes 294944 | tf_op jit(solution)/shard_map/all_to_all | solution.py:206
  (92 shorter events, 35.9 us)
Async XLA Ops:
  0.6 4.0 %copy-start.7 = (bf16[288,512]{1,0:T(8,128)(2,1)S(1)}, bf16[288,512]{1,0:T(8,128)(2,1)}, u32[]{:S(2)}) copy-start(bf16[288,512]{1,0:T(8,128)(2,1)} %param.6) | copy-start | bytes 884740
  3.1 17.4 %copy-start.6 = (bf16[4,288,288]{2,1,0:T(8,128)(2,1)S(1)}, bf16[4,288,288]{2,1,0:T(8,128)(2,1)}, u32[]{:S(2)}) copy-start(bf16[4,288,288]{2,1,0:T(8,128)(2,1)} %param.7) | copy-start | bytes 1990660
  5.5 34.2 %all-to-all-start = ((bf16[4,80,512]{2,1,0:T(8,128)(2,1)}), bf16[4,80,512]{2,1,0:T(8,128)(2,1)S(1)}, u32[]{:S(2)}, u32[]{:S(2)}) async-start(bf16[4,80,512]{2,1,0:T(8,128)(2,1)} %maximum_maximum_fusion.1), calls=%async_computation | async-start | bytes 655360 | tf_op jit(solution)/shard_map/all_to_all | solution.py:339
  22.5 15.2 %collective-permute-start.2 = (bf16[2,4,72,288]{3,2,1,0:T(8,128)(2,1)}, bf16[2,4,72,288]{3,2,1,0:T(8,128)(2,1)S(1)}, u32[]{:S(2)}, u32[]{:S(2)}) collective-permute-start(bf16[2,4,72,288]{3,2,1,0:T(8,128)(2,1)} %get-tuple-element.58), channel_id=1, source_target_pairs={{0,2},{1,3},{2,0},{3,1},{4,6},{5,7},{6,4},{7,5},{8,10},{9,11},{10,... | collective-permute-start | bytes 995336 | tf_op jit(solution)/shard_map/ppermute | solution.py:279
  30.6 5.5 %collective-permute-start.1 = (bf16[32,128]{1,0:T(8,128)(2,1)S(1)}, bf16[32,128]{1,0:T(8,128)(2,1)S(1)}, u32[]{:S(2)}, u32[]{:S(2)}) collective-permute-start(bf16[32,128]{1,0:T(8,128)(2,1)S(1)} %get-tuple-element.64), channel_id=1, source_target_pairs={{0,128},{128,256},{256,384},{384,0},{1,129},{129,257},{257,385},{3... | collective-permute-start | bytes 24584 | tf_op jit(solution)/shard_map/ppermute | solution.py:279
  37.8 1.9 %copy-start.9 = (bf16[2,4,72,288]{3,2,1,0:T(8,128)(2,1)}, bf16[2,4,72,288]{3,2,1,0:T(8,128)(2,1)S(1)}, u32[]{:S(2)}) copy-start(bf16[2,4,72,288]{3,2,1,0:T(8,128)(2,1)S(1)} %collective-permute-done.2) | copy-start | bytes 995332
  39.7 8.5 %copy-start.11 = (s32[2,512]{1,0:T(2,128)S(1)}, s32[2,512]{1,0:T(2,128)}, u32[]{:S(2)}) copy-start(s32[2,512]{1,0:T(2,128)} %param.11) | copy-start | bytes 12292
  40.9 7.9 %copy-start.8 = (bf16[2,4,72,288]{3,2,1,0:T(8,128)(2,1)S(1)}, bf16[2,4,72,288]{3,2,1,0:T(8,128)(2,1)}, u32[]{:S(2)}) copy-start(bf16[2,4,72,288]{3,2,1,0:T(8,128)(2,1)} %get-tuple-element.32) | copy-start | bytes 995332
  40.9 37.6 %all-to-all-start.1 = ((bf16[4,4,80,512]{3,2,1,0:T(8,128)(2,1)}), bf16[4,4,80,512]{3,2,1,0:T(8,128)(2,1)S(1)}, u32[]{:S(2)}, u32[]{:S(2)}) async-start(bf16[4,4,80,512]{3,2,1,0:T(8,128)(2,1)} %broadcast_in_dim.63), calls=%async_computation.1 | async-start | bytes 2621440 | tf_op jit(solution)/shard_map/all_to_all | solution.py:170
  48.8 17.2 %collective-permute-start.5 = (bf16[2,4,72,288]{3,2,1,0:T(8,128)(2,1)S(1)}, bf16[2,4,72,288]{3,2,1,0:T(8,128)(2,1)S(1)}, u32[]{:S(2)}, u32[]{:S(2)}) collective-permute-start(bf16[2,4,72,288]{3,2,1,0:T(8,128)(2,1)S(1)} %copy-done.8), channel_id=1, source_target_pairs={{0,1},{1,2},{2,3},{3,0},{4,5},{5,6},{6,7},{7,4},{8,9},{9,10},{10,1... | collective-permute-start | bytes 995336 | tf_op jit(solution)/shard_map/ppermute | solution.py:279
  52.3 13.7 %collective-permute-start.6 = (bf16[2,4,72,288]{3,2,1,0:T(8,128)(2,1)S(1)}, bf16[2,4,72,288]{3,2,1,0:T(8,128)(2,1)}, u32[]{:S(2)}, u32[]{:S(2)}) collective-permute-start(bf16[2,4,72,288]{3,2,1,0:T(8,128)(2,1)S(1)} %get-tuple-element.34), channel_id=1, source_target_pairs={{0,3},{1,0},{2,1},{3,2},{4,7},{5,4},{6,5},{7,6},{8,11},{9,8},{10,9... | collective-permute-start | bytes 995336 | tf_op jit(solution)/shard_map/ppermute | solution.py:279
  56.0 7.8 %collective-permute-start.3 = (bf16[32,128]{1,0:T(8,128)(2,1)S(1)}, bf16[32,128]{1,0:T(8,128)(2,1)S(1)}, u32[]{:S(2)}, u32[]{:S(2)}) collective-permute-start(bf16[32,128]{1,0:T(8,128)(2,1)S(1)} %get-tuple-element.29), channel_id=1, source_target_pairs={{0,256},{128,384},{256,0},{384,128},{1,257},{129,385},{257,1},{385... | collective-permute-start | bytes 24584 | tf_op jit(solution)/shard_map/ppermute | solution.py:279
  59.3 6.8 %collective-permute-start.4 = (bf16[32,128]{1,0:T(8,128)(2,1)S(1)}, bf16[32,128]{1,0:T(8,128)(2,1)S(1)}, u32[]{:S(2)}, u32[]{:S(2)}) collective-permute-start(bf16[32,128]{1,0:T(8,128)(2,1)S(1)} %get-tuple-element.30), channel_id=1, source_target_pairs={{0,384},{128,0},{256,128},{384,256},{1,385},{129,1},{257,129},{385... | collective-permute-start | bytes 24584 | tf_op jit(solution)/shard_map/ppermute | solution.py:279
  61.9 20.2 %collective-permute-start = (f32[4,289]{0,1:T(8,128)}, f32[4,289]{0,1:T(8,128)}, u32[]{:S(2)}, u32[]{:S(2)}) collective-permute-start(f32[4,289]{0,1:T(8,128)} %pad_maximum_fusion.1), channel_id=1, source_target_pairs={{0,4},{4,8},{8,12},{12,16},{16,20},{20,24},{24,28},{28,32},{32,36}... | collective-permute-start | bytes 13880 | tf_op jit(solution)/shard_map/ppermute | solution.py:45
  79.4 30.1 %collective-permute-start.7 = (bf16[16,80,512]{2,1,0:T(8,128)(2,1)S(1)}, bf16[16,80,512]{2,1,0:T(8,128)(2,1)}, u32[]{:S(2)}, u32[]{:S(2)}) collective-permute-start(bf16[16,80,512]{2,1,0:T(8,128)(2,1)S(1)} %bitcast.80), channel_id=1, source_target_pairs={{0,4},{4,0},{1,5},{5,1},{2,6},{6,2},{3,7},{7,3},{8,12},{12,8},{9,1... | collective-permute-start | bytes 3932168 | tf_op jit(solution)/shard_map/ppermute | solution.py:165
  85.1 13.0 %all-to-all-start.2 = ((bf16[8,192,128]{2,1,0:T(8,128)(2,1)}), bf16[8,192,128]{2,1,0:T(8,128)(2,1)}, u32[]{:S(2)}, u32[]{:S(2)}) async-start(bf16[8,192,128]{2,1,0:T(8,128)(2,1)} %bitcast.42), calls=%async_computation.2 | async-start | bytes 786432 | tf_op jit(solution)/shard_map/all_to_all | solution.py:309
  90.8 1.5 copy-start.1
  102.7 32.4 %all-to-all-start.3 = ((bf16[16,72,128]{2,1,0:T(8,128)(2,1)}), bf16[16,72,128]{2,1,0:T(8,128)(2,1)S(1)}, u32[]{:S(2)}, u32[]{:S(2)}) async-start(bf16[16,72,128]{2,1,0:T(8,128)(2,1)} %broadcast_in_dim.60), calls=%async_computation.3 | async-start | bytes 589824 | tf_op jit(solution)/shard_map/all_to_all | solution.py:360
  134.0 1.0 copy-start
  135.0 9.6 %copy-start.2 = (s32[32,1024]{1,0:T(8,128)S(1)}, s32[32,1024]{1,0:T(8,128)}, u32[]{:S(2)}) copy-start(s32[32,1024]{1,0:T(8,128)} %get-tuple-element.46.refs_4_) | copy-start | bytes 393220
  135.0 9.6 %copy-start.3 = (s32[128,256]{1,0:T(8,128)S(1)}, s32[128,256]{1,0:T(8,128)}, u32[]{:S(2)}) copy-start(s32[128,256]{1,0:T(8,128)} %get-tuple-element.47.refs_5_) | copy-start | bytes 393220
  135.0 22.5 %all-to-all-start.4 = ((bf16[16,72,512]{2,1,0:T(8,128)(2,1)}), bf16[16,72,512]{2,1,0:T(8,128)(2,1)}, u32[]{:S(2)}, u32[]{:S(2)}) async-start(bf16[16,72,512]{2,1,0:T(8,128)(2,1)} %bitcast.82), calls=%async_computation.4 | async-start | bytes 2359296 | tf_op jit(solution)/shard_map/all_to_all | solution.py:206
  141.2 3.5 %collective-permute-start.8 = (bf16[16,72,128]{2,1,0:T(8,128)(2,1)S(1)}, bf16[16,72,128]{2,1,0:T(8,128)(2,1)S(1)}, u32[]{:S(2)}, u32[]{:S(2)}) collective-permute-start(bf16[16,72,128]{2,1,0:T(8,128)(2,1)S(1)} %all-to-all-done.3.refs_2_), channel_id=1, source_target_pairs={{0,4},{4,0},{1,5},{5,1},{2,6},{6,2},{3,7},{7,3},{8,12},{12,8},{9,1... | collective-permute-start | bytes 884744 | tf_op jit(solution)/shard_map/ppermute | solution.py:165
  157.5 13.7 %all-to-all-start.5 = ((bf16[16,72,128]{2,1,0:T(8,128)(2,1)}), bf16[16,72,128]{2,1,0:T(8,128)(2,1)S(1)}, u32[]{:S(2)}, u32[]{:S(2)}) async-start(bf16[16,72,128]{2,1,0:T(8,128)(2,1)} %bitcast.48), calls=%async_computation.5 | async-start | bytes 589824 | tf_op jit(solution)/shard_map/all_to_all | solution.py:206
  (3 other events, 2.6 us)
